TPU v7x, 128 devices: a whole 4x4x4 slice. The times are simulated.
128 devices in a mesh: dom: 8 (over z, core), ml: 16 (over x, y).
Axes of the slice: x: 4, y: 4, z: 4, core: 2. Of those that a mesh axis runs over, the one named last changes fastest.
Arguments:
- mm_positions: float32 [3, 262144], P(None, ('dom', 'ml')), may hold values from -6 to 6
- mm_charge: float32 [262144], P(('dom', 'ml')), may hold values from -1 to 1
- mm_tiles: int32 [2048, 8], P(('dom', 'ml')), may hold values from 0 to 47, as said below
- ml_feat: bfloat16 [64, 512, 128], P('dom', 'ml'), may hold values from -6 to 6
- ml_positions: float32 [64, 3, 512], P('dom', None, 'ml'), may hold values from -6 to 6
- ml_neighbours: int32 [64, 32, 512], P('dom', None, 'ml'), may hold values from 0 to 511
- msg_weight: bfloat16 [2, 128, 128], replicated, may hold values from -0.5 to 0.5
- radial_weight: float32 [2, 8, 128], replicated, may hold values from -5 to 5
- out_weight: bfloat16 [2, 128, 128], replicated, may hold values from -0.5 to 0.5
- read_weight: bfloat16 [128, 256], replicated, may hold values from -0.5 to 0.5
Outputs:
- mm_force: float32 [3, 262144], P(None, ('dom', 'ml'))
- ml_force: float32 [64, 3, 512], P('dom', None, 'ml')
Inputs may be any that keep to these rules, and one draw needn't show every extreme that they name: `mm_tiles`: for each tile of a device, 8 distinct positions among the 16 tiles of the previous device along dom+ml (wrapping), its own tiles and the next device's, in that order; at least one lies among the previous device's tiles and at least one among the next device's. `ml_neighbours`: indices of atoms within the same patch.
All inputs are finite; a program needn't handle non-finite values.
Results may differ from a plain program's by a relative error of at most 0.007.
Values may be sent and summed in bfloat16 or wider, within the bound.
No kernel may reach another device: no remote copies, remote signals or barrier semaphores. Data moves between devices by JAX's collectives and lax.ppermute only.
A program may use at most 320 MiB of HBM per device.

v0:
```python
import math

import jax
import jax.numpy as jnp
from jax import lax
from jax.sharding import PartitionSpec as P

TILE = 128


RADIUS = 6.0
SOFTEN = 1.0
COULOMB = 0.5


def padded(block, sides, width):
    for axis, dim in sides:
        count = lax.axis_size(axis)
        forward = [(i, i + 1) for i in range(count - 1)]
        forward.append((count - 1, 0))
        backward = [(target, source) for source, target in forward]
        low = lax.ppermute(
            lax.slice_in_dim(block, block.shape[dim] - width, None, axis=dim), axis, forward
        )
        high = lax.ppermute(lax.slice_in_dim(block, 0, width, axis=dim), axis, backward)
        block = jnp.concatenate([low, block, high], axis=dim)
    return block


def pair_force(own_tile, near_tiles):
    offsets = own_tile[:3, None, :, None] - near_tiles[:3, :, None, :]
    squared = jnp.sum(offsets * offsets, axis=0) + SOFTEN
    inverse = 1.0 / (squared * jnp.sqrt(squared))
    strength = COULOMB * own_tile[3][None, :, None] * near_tiles[3][:, None, :] * inverse
    return jnp.sum(strength[None] * offsets, axis=(1, 3))


def slot_forces(
    hidden,
    own_positions,
    neighbours,
    all_positions,
    msg_weight,
    radial_weight,
    out_weight,
    read_weight,
):
    offsets = (
        jax.vmap(lambda table_part, index_part: table_part[:, index_part])(
            all_positions, neighbours
        )
        - own_positions[:, :, None, :]
    )
    distance = jnp.sqrt(jnp.sum(offsets * offsets, axis=1) + 1.0)
    envelope = 0.5 * (jnp.cos(jnp.pi * jnp.minimum(distance / RADIUS, 1.0)) + 1.0)
    basis_count = radial_weight.shape[1]
    centers = jnp.arange(basis_count).astype(jnp.float32) * (RADIUS / basis_count)
    radial_basis = (
        jnp.exp(-2.0 * (distance[:, None] - centers[None, :, None, None]) ** 2) * envelope[:, None]
    )
    norm_factor = 1.0 / math.sqrt(neighbours.shape[1])
    channel_count = hidden.shape[2]
    for layer_index in range(msg_weight.shape[0]):
        mixed_feat = jnp.einsum(
            "rqc,cd->rqd", hidden, msg_weight[layer_index], preferred_element_type=jnp.float32
        ).astype(jnp.bfloat16)
        sender_feat = lax.all_gather(mixed_feat, "ml", axis=1, tiled=True)
        radial_map = radial_weight[layer_index]

        def slot_message(pieces):
            table_part, index_part, basis_part = pieces
            radial = jnp.einsum(
                "nkq,nc->kqc", basis_part, radial_map, precision=lax.Precision.HIGHEST
            )
            return (
                jnp.sum(radial * table_part[index_part].astype(jnp.float32), axis=0) * norm_factor
            )

        message = lax.map(slot_message, (sender_feat, neighbours, radial_basis))
        active = jax.nn.silu(message).astype(jnp.bfloat16)
        update = jnp.einsum(
            "rqc,cd->rqd", active, out_weight[layer_index], preferred_element_type=jnp.float32
        )
        hidden = (hidden.astype(jnp.float32) + update).astype(jnp.bfloat16)
    readout = jnp.einsum(
        "rqc,cd->rqd", hidden, read_weight, preferred_element_type=jnp.float32
    ).astype(jnp.bfloat16)
    query_feat = readout[:, :, :channel_count]
    key_feat = readout[:, :, channel_count:]
    gathered_keys = lax.all_gather(key_feat, "ml", axis=1, tiled=True)

    def slot_pull(pieces):
        query_part, table_part, index_part, envelope_part, offset_part = pieces
        strength = (
            jnp.einsum(
                "qc,kqc->kq", query_part, table_part[index_part], preferred_element_type=jnp.float32
            )
            / channel_count
            * envelope_part
        )
        return jnp.sum(strength[None] * offset_part, axis=1)

    return lax.map(slot_pull, (query_feat, gathered_keys, neighbours, envelope, offsets))


def on_device(
    mm_positions,
    mm_charge,
    mm_tiles,
    ml_feat,
    ml_positions,
    ml_neighbours,
    msg_weight,
    radial_weight,
    out_weight,
    read_weight,
):
    patch_count = ml_feat.shape[0]
    domain_count = lax.axis_size("dom")
    capacity = max(2, 2 * patch_count // domain_count)
    slot_count = domain_count * capacity
    patch_order = jnp.arange(patch_count, dtype=jnp.int32)
    target_group = (
        lax.axis_index("dom") - 1 + patch_order * (domain_count // 2 + 1)
    ) % domain_count
    earlier_same = (target_group[None, :] == target_group[:, None]) & (
        patch_order[None, :] < patch_order[:, None]
    )
    slot_index = target_group * capacity + jnp.sum(earlier_same.astype(jnp.int32), axis=1)
    slot_match = slot_index[None, :] == jnp.arange(slot_count, dtype=jnp.int32)[:, None]
    source = jnp.sum(jnp.where(slot_match, patch_order[None, :], 0), axis=1)
    geometry = jnp.concatenate([ml_positions, ml_neighbours.astype(jnp.float32)], axis=1)
    feat_sent = jnp.take(ml_feat, source, axis=0)
    geometry_sent = jnp.take(geometry, source, axis=0)
    feat_recv = lax.all_to_all(feat_sent, "dom", split_axis=0, concat_axis=0, tiled=True)
    geometry_recv = lax.all_to_all(geometry_sent, "dom", split_axis=0, concat_axis=0, tiled=True)
    mm_atoms = jnp.concatenate([mm_positions, mm_charge[None]], axis=0)
    atom_count = mm_atoms.shape[1]
    tile_count = atom_count // TILE
    window_atoms = padded(mm_atoms, ((("dom", "ml"), 1),), atom_count)
    window_tiles = window_atoms.reshape(4, 3 * tile_count, TILE)
    own_tiles = mm_atoms.reshape(4, tile_count, TILE).transpose(1, 0, 2)

    def tile_force(pieces):
        own_tile, tile_list = pieces
        return pair_force(own_tile, window_tiles[:, tile_list])

    mm_force = lax.map(tile_force, (own_tiles, mm_tiles)).transpose(1, 0, 2).reshape(3, atom_count)
    own_positions = geometry_recv[:, :3]
    all_positions = lax.all_gather(own_positions, "ml", axis=2, tiled=True)
    neighbours = geometry_recv[:, 3:].astype(jnp.int32)
    forces = slot_forces(
        feat_recv,
        own_positions,
        neighbours,
        all_positions,
        msg_weight,
        radial_weight,
        out_weight,
        read_weight,
    )
    returned = lax.all_to_all(forces, "dom", split_axis=0, concat_axis=0, tiled=True)
    ml_force = jnp.take(returned, slot_index, axis=0)
    return (mm_force, ml_force)


def solution(mesh):
    in_specs = (
        P(None, ("dom", "ml")),
        P(("dom", "ml")),
        P(("dom", "ml"), None),
        P("dom", "ml", None),
        P("dom", None, "ml"),
        P("dom", None, "ml"),
        P(),
        P(),
        P(),
        P(),
    )
    out_specs = (P(None, ("dom", "ml")), P("dom", None, "ml"))
    return jax.shard_map(
        on_device, mesh=mesh, in_specs=in_specs, out_specs=out_specs, check_vma=False
    )
```

profile of v0, /device:TPU:0, one launch (start us, length us, event | category | flops | bytes accessed | tf_op | source)
XLA Modules:
  0.0 723.6 jit_solution(11271315500389507158)
XLA Ops:
  9.5 11.3 %all_to_all.15 = bf16[16,32,128]{2,1,0:T(8,128)(2,1)S(1)} all-to-all(bf16[16,32,128]{2,1,0:T(8,128)(2,1)S(1)} %broadcast_select_fusion.1), channel_id=1, replica_groups=mesh['dom'=8,'ml'=16] {'dom'}, dimensions={0} | all-to-all | bytes 262144 | tf_op jit(solution)/shard_map/all_to_all | solution.py:135
  26.0 3.4 all-to-all-start.1
  29.4 5.5 all-to-all-done.1
  37.2 43.4 %all_gather.12 = f32[16,3,512]{1,2,0:T(8,128)} all-gather(f32[16,3,32]{1,2,0:T(8,128)S(1)} %bitcast.199), channel_id=1, replica_groups=mesh['dom'=8,'ml'=16] {'ml'}, dimensions={2}, use_global_device_ids=true | all-gather | bytes 104448 | tf_op jit(solution)/shard_map/all_gather | solution.py:150
  80.5 236.4 %gather_fusion.7 = f32[16384,3]{1,0:T(8,128)} fusion(f32[16,3,512]{1,2,0:T(8,128)} %all_gather.12, s32[16384]{0:T(1024)S(1)} %reshape.355), kind=kCustom, calls=%fused_computation.7 | custom fusion | bytes 524288 | tf_op jit(solution)/shard_map/vmap()/gather | solution.py:49
  316.9 6.0 copy.38
  325.8 84.9 %while.41 = (s32[]{:T(128)}, f32[16,32,128]{2,1,0:T(8,128)S(1)}, f32[16,8,32,32]{3,1,2,0:T(8,128)S(1)}, f32[8,128]{1,0:T(8,128)S(1)}, bf16[16,512,128]{2,1,0:T(8...) while((s32[]{:T(128)}, f32[16,32,128]{2,1,0:T(8,128)S(1)}, f32[16,8,32,32]{3,1,2,0:T(8,128)S(1)}, ...), condition=%wide.region_9.10_spmd, body=%wide.region_7.9_spmd.sunk | while | flops 12980226 | bytes 1261661 | solution.py:79
  337.5 3.2 gather_fusion.1
  342.8 3.2 gather_fusion.1
  374.6 3.2 gather_fusion.1
  390.5 3.2 gather_fusion.1
  395.8 3.2 gather_fusion.1
  401.1 3.2 gather_fusion.1
  412.5 44.6 %all-gather.6.cloned.1.call-done = bf16[16,512,128]{2,1,0:T(8,128)(2,1)} async-done(((bf16[16,32,128]{2,1,0:T(8,128)(2,1)}), bf16[16,512,128]{2,1,0:T(8,128)(2,1)}) %all-gather.6.cloned.1.call-update) | async-done | bytes 2097168 | tf_op jit(solution)/shard_map/all_gather | solution.py:67
  457.2 84.9 %while.42 = (s32[]{:T(128)}, f32[16,32,128]{2,1,0:T(8,128)S(1)}, f32[16,8,32,32]{3,1,2,0:T(8,128)S(1)}, f32[8,128]{1,0:T(8,128)S(1)}, bf16[16,512,128]{2,1,0:T(8...) while((s32[]{:T(128)}, f32[16,32,128]{2,1,0:T(8,128)S(1)}, f32[16,8,32,32]{3,1,2,0:T(8,128)S(1)}, ...), condition=%wide.region_12.13_spmd, body=%wide.region_10.12_spmd.sunk | while | flops 12980226 | bytes 1261661 | solution.py:79
  468.9 3.2 gather_fusion.2
  474.2 3.2 gather_fusion.2
  506.0 3.2 gather_fusion.2
  521.9 3.2 gather_fusion.2
  527.2 3.2 gather_fusion.2
  532.5 3.2 gather_fusion.2
  544.5 6.0 collective-permute-start.1
  552.2 38.2 %all-gather.8.cloned.1.call-done = bf16[16,512,128]{2,1,0:T(8,128)(2,1)} async-done(((bf16[16,32,128]{2,1,0:T(8,128)(2,1)}), bf16[16,512,128]{2,1,0:T(8,128)(2,1)}) %all-gather.8.cloned.1.call-update) | async-done | bytes 2097168 | tf_op jit(solution)/shard_map/all_gather | solution.py:90
  590.4 87.1 %while.43 = (s32[]{:T(128)}, f32[16,3,32]{2,1,0:T(4,128)S(1)}, bf16[16,512,128]{2,1,0:T(8,128)(2,1)}, s32[16,32,32]{2,1,0:T(8,128)S(1)}, bf16[16,32,128]{2,1,0:T...) while((s32[]{:T(128)}, f32[16,3,32]{2,1,0:T(4,128)S(1)}, ...), condition=%wide.region_15.16_spmd, body=%wide.region_13.15_spmd.sunk | while | flops 274338 | bytes 1147373 | solution.py:103
  591.4 3.2 gather_fusion.3
  602.3 3.2 gather_fusion.3
  607.7 3.2 gather_fusion.3
  656.7 3.2 gather_fusion.3
  662.2 3.2 gather_fusion.3
  667.6 3.2 gather_fusion.3
  678.2 4.4 all-to-all-start.2
  682.6 32.5 %while.40 = (s32[]{:T(128)}, f32[16,3,128]{2,1,0:T(4,128)}, f32[16,4,128]{2,1,0:T(4,128)S(1)}, s32[16,8]{1,0:T(8,128)S(1)}, f32[4,48,128]{2,0,1:T(4,128)S(1)}, /*index=5*/s32[]{:T(128)}) while((s32[]{:T(128)}, f32[16,3,128]{2,1,0:T(4,128)}, f32[16,4,128]{2,1,0:T(4,128)S(1)}, s32[16,8]{1,0:T(8,128)S(1)}, f32[4,48,128]{2,0,1:T(4,128)S(1)}, ...), condition=%wide.region_3.4_spmd, body=%wide.region_0.0_spmd.sunk | while | flops 2884378 | bytes 2213069 | solution.py:148
  (654 shorter events, 249.1 us)
Async XLA Ops:
  7.2 535.0 %copy-start = (bf16[128,256]{1,0:T(8,128)(2,1)S(1)}, bf16[128,256]{1,0:T(8,128)(2,1)}, u32[]{:S(2)}) copy-start(bf16[128,256]{1,0:T(8,128)(2,1)} %param.27) | copy-start | bytes 196612
  7.2 22.2 %copy-start.4 = (f32[2,8,128]{2,1,0:T(8,128)S(1)}, f32[2,8,128]{2,1,0:T(8,128)}, u32[]{:S(2)}) copy-start(f32[2,8,128]{2,1,0:T(8,128)} %param.25) | copy-start | bytes 24580
  7.2 318.6 %all-gather.4.cloned.1.call-start = ((), (), s32[]{:S(2)}) async-start(), calls=%async_computation.3 | async-start | bytes 2228224 | tf_op jit(solution)/shard_map/all_gather | solution.py:67
  7.4 0.5 copy-start.6
  26.0 8.9 %all-to-all-start.1 = ((f32[8,1,2240]{2,1,0:T(1,128)}), f32[8,1,2240]{2,1,0:T(1,128)S(1)}, u32[]{:S(2)}, u32[]{:S(2)}) async-start(f32[8,1,2240]{2,1,0:T(1,128)} %reshape.380), calls=%async_computation.1 | async-start | bytes 147456 | tf_op jit(solution)/shard_map/all_to_all | solution.py:136
  29.3 427.9 %all-gather.6.cloned.1.call-start = ((), (), s32[]{:S(2)}) async-start(), calls=%async_computation.4 | async-start | bytes 2228224 | tf_op jit(solution)/shard_map/all_gather | solution.py:67
  325.8 85.8 %copy-start.3 = (bf16[2,128,128]{2,1,0:T(8,128)(2,1)S(1)}, bf16[2,128,128]{2,1,0:T(8,128)(2,1)}, u32[]{:S(2)}) copy-start(bf16[2,128,128]{2,1,0:T(8,128)(2,1)} %param.24) | copy-start | bytes 196612
  412.5 177.9 %all-gather.8.cloned.1.call-start = ((), (), s32[]{:S(2)}) async-start(), calls=%async_computation.5 | async-start | bytes 2228224 | tf_op jit(solution)/shard_map/all_gather | solution.py:90
  457.2 84.9 %copy-start.8 = (bf16[2,128,128]{2,1,0:T(8,128)(2,1)S(1)}, bf16[2,128,128]{2,1,0:T(8,128)(2,1)}, u32[]{:S(2)}) copy-start(bf16[2,128,128]{2,1,0:T(8,128)(2,1)} %param.26) | copy-start | bytes 196612
  542.1 1.2 copy-start.1
  542.1 1.2 copy-start.2
  542.1 8.5 %copy-start.7 = (s32[8]{0:T(128)S(1)}, s32[8]{0:T(128)}, u32[]{:S(2)}) copy-start(s32[8]{0:T(128)} %copy-done.6) | copy-start | bytes 100
  542.1 8.5 %copy-start.5 = (s32[16,8]{0,1:T(8,128)S(1)}, s32[16,8]{0,1:T(8,128)}, u32[]{:S(2)}) copy-start(s32[16,8]{0,1:T(8,128)} %param.20) | copy-start | bytes 1540
  543.3 8.8 %collective-permute-start = (f32[4,2048]{1,0:T(4,128)S(1)}, f32[4,2048]{1,0:T(4,128)S(1)}, u32[]{:S(2)}, u32[]{:S(2)}) collective-permute-start(f32[4,2048]{1,0:T(4,128)S(1)} %pad_maximum_fusion.1), channel_id=1, source_target_pairs={{0,1},{1,2},{2,3},{3,4},{4,5},{5,6},{6,7},{7,8},{8,9},{9,10},{10,1... | collective-permute-start | bytes 98312 | tf_op jit(solution)/shard_map/ppermute | solution.py:22
  544.5 7.6 %collective-permute-start.1 = (f32[4,2048]{1,0:T(4,128)S(1)}, f32[4,2048]{1,0:T(4,128)S(1)}, u32[]{:S(2)}, u32[]{:S(2)}) collective-permute-start(f32[4,2048]{1,0:T(4,128)S(1)} %pad_maximum_fusion.1), channel_id=1, source_target_pairs={{1,0},{2,1},{3,2},{4,3},{5,4},{6,5},{7,6},{8,7},{9,8},{10,9},{11,1... | collective-permute-start | bytes 98312 | tf_op jit(solution)/shard_map/ppermute | solution.py:25
  678.2 36.9 %all-to-all-start.2 = ((f32[8,1,192]{2,1,0:T(1,128)}), f32[8,1,192]{2,1,0:T(1,128)S(1)}, u32[]{:S(2)}, u32[]{:S(2)}) async-start(f32[8,1,192]{2,1,0:T(1,128)} %reshape.382), calls=%async_computation.2 | async-start | bytes 16384 | tf_op jit(solution)/shard_map/all_to_all | solution.py:162
Sparse Core Ops, SparseCore 0:
  22.6 55.9 all-gather.3
  412.6 44.5 all-gather.5
  543.4 46.9 all-gather.7
where the time goes:
time: 729 us; the launch traced here: 724 us
  local copies, waits for them, and re-layouts  473 us (65%)
  waiting for transfers between devices  89.8 us (12%)
  blocking collectives  54.7 us (8%)
  matrix products  40.6 us (6%)
  other arithmetic  32.4 us (4%)
  starting transfers between devices  15.1 us (2%)
  between operations  14.1 us (2%)
    gather x4, local copies, waits for them, and re-layouts, slot_forces(): table_part[:, index_part]  243 us
    gather x32, local copies, waits for them, and re-layouts, slot_message(): table_part[index_part].astype(jnp.float32)  102 us
    gather x16, local copies, waits for them, and re-layouts, slot_pull(): table_part[index_part]  51.2 us
    all_gather x2, waiting for transfers between devices, slot_forces(): sender_feat = lax.all_gather(mixed_feat, 'ml', axis=1, tiled=True)  44.7 us
    squeeze x48, local copies, waits for them, and re-layouts, slot_forces(): message = lax.map(slot_message, (sender_feat, neighbours, radial_basis))  44.1 us
    all_gather x1, blocking collectives, on_device(): all_positions = lax.all_gather(own_positions, 'ml', axis=2, tiled=True)  43.4 us
    all_gather x1, waiting for transfers between devices, slot_forces(): gathered_keys = lax.all_gather(key_feat, 'ml', axis=1, tiled=True)  38.2 us
    dot_general x32, matrix products, slot_message(): jnp.einsum('nkq,nc->kqc', basis_part, radial_map, precision=lax.Precision...  33 us
  transfers between devices with their start and end apart: 7, of which 4 were waited for; matrix products, arithmetic and copies ran while one was open for 39% of the time, Pallas kernels for 0%

commit v1 on v0

v1 whole, which is shorter than its diff:
```python
import math

import jax
import jax.numpy as jnp
from jax import lax
from jax.experimental import pallas as pl
from jax.experimental.pallas import tpu as pltpu
from jax.sharding import PartitionSpec as P

TILE = 128
RADIUS = 6.0
SOFTEN = 1.0
COULOMB = 0.5
HALVES = 2

COSINE = (
    0.9999999991255941,
    -0.23370050635000697,
    0.019968606683524803,
    -0.0008935362638784474,
    2.3601070666008123e-05,
)

F32 = jnp.float32
BF16 = jnp.bfloat16


def pack_kernel(feat_ref, pos_ref, nb_ref, mm_pos_ref, mm_charge_ref, send_ref, atoms_ref, geo_ref):
    patches, atoms, _ = feat_ref.shape
    geo_ref[...] = jnp.zeros_like(geo_ref)
    for p in range(patches):
        numbers = (nb_ref[p] - 256).astype(F32)
        geo_ref[p, 0:16, 0:32] = numbers[0:16]
        geo_ref[p, 0:16, 32:64] = numbers[16:32]
        place = pos_ref[p]
        high = place.astype(BF16).astype(F32)
        rest = place - high
        middle = rest.astype(BF16).astype(F32)
        geo_ref[p, 0:3, 64:96] = high
        geo_ref[p, 0:3, 96:128] = middle
        geo_ref[p, 8:11, 64:96] = rest - middle
        block = geo_ref[p].astype(BF16)
        for half in range(HALVES):
            send_ref[half * patches + p, 0:atoms, :] = feat_ref[p]
            send_ref[half * patches + p, atoms : atoms + 16, :] = block
    atoms_ref[0:3, :] = mm_pos_ref[...]
    atoms_ref[3:4, :] = mm_charge_ref[...]


def patch_kernel(
    half_ref,
    recv_ref,
    msg_ref,
    radial_ref,
    out_w_ref,
    read_ref,
    force_ref,
    hidden_ref,
    pos_ref,
    place_ref,
    low_ref,
    unit_ref,
    count_ref,
    basis_ref,
    pull_ref,
    next_ref,
):
    sources = recv_ref.shape[0]
    share = recv_ref.shape[1] - 16
    size = sources * share
    own = size // HALVES
    neighbours = low_ref.shape[0]
    basis_count = radial_ref.shape[1]
    layers = msg_ref.shape[0]
    channels = recv_ref.shape[2]

    for m in range(sources):
        hidden_ref[share * m : share * (m + 1), :] = recv_ref[m, 0:share, :]
        geo = recv_ref[m, share : share + 16, :].astype(F32)
        lanes = slice(share * m, share * (m + 1))
        pos_ref[:, lanes] = (geo[0:8, 64:96] + geo[0:8, 96:128]) + geo[8:16, 64:96]
        low_ref[0:16, lanes] = geo[:, 0:32].astype(jnp.int32) + 256
        low_ref[16:32, lanes] = geo[:, 32:64].astype(jnp.int32) + 256
    place_ref[...] = jnp.transpose(pos_ref[...])
    index = low_ref[...]
    low_ref[...] = index & 127
    unit_ref[...] = jnp.int32(1) << ((index >> 7) << 3)

    rows = lax.broadcasted_iota(jnp.int32, (128, 128), 0)
    for block in range(size // 128):
        lanes = slice(128 * block, 128 * (block + 1))
        total = jnp.zeros((128, 128), jnp.int32)
        for k in range(neighbours):
            total += jnp.where(rows == low_ref[k : k + 1, lanes], unit_ref[k : k + 1, lanes], 0)
        count_ref[lanes, :] = jnp.transpose(total)

    step = 16

    def pairs(block, carry):
        own_rows = pl.ds(pl.multiple_of(block * step, step), step)
        squared = SOFTEN
        for axis in range(3):
            offset = pos_ref[axis : axis + 1, :] - place_ref[own_rows, axis : axis + 1]
            squared = offset * offset + squared
        packed = count_ref[own_rows, :]
        times = jnp.concatenate(
            [(packed >> (8 * f)) & 255 for f in range(size // 128)], axis=1
        ).astype(F32)
        near = jnp.minimum(squared, RADIUS * RADIUS)
        u = near * (1.0 / (RADIUS * RADIUS))
        series = COSINE[4]
        for value in COSINE[3::-1]:
            series = series * u + value
        root = (1.0 - u) * series
        envelope = root * root * times
        pull_ref[own_rows, :] = envelope
        distance = near * lax.rsqrt(near)
        growth = jnp.exp(distance * (4.0 * RADIUS / basis_count))
        basis = jnp.exp(near * -2.0) * envelope
        for n in range(basis_count):
            basis_ref[n, own_rows, :] = basis.astype(BF16)
            if n + 1 < basis_count:
                basis = basis * growth
        return carry

    lax.fori_loop(0, size // step, pairs, 0)

    number = lax.broadcasted_iota(jnp.int32, (basis_count, channels), 0).astype(F32)
    center = number * (RADIUS / basis_count)
    scale = jnp.exp(center * center * -2.0) * (1.0 / math.sqrt(neighbours))
    chunk = 256
    for layer in range(layers):
        mixed = jnp.dot(
            hidden_ref[...], msg_ref[layer], preferred_element_type=F32
        ).astype(BF16)
        radial = radial_ref[layer] * scale
        for block in range(size // chunk):
            part = slice(chunk * block, chunk * (block + 1))
            message = jnp.zeros((chunk, channels), F32)
            for n in range(basis_count):
                message += radial[n : n + 1, :] * jnp.dot(
                    basis_ref[n, part, :], mixed, preferred_element_type=F32
                )
            active = jax.nn.silu(message).astype(BF16)
            update = jnp.dot(active, out_w_ref[layer], preferred_element_type=F32)
            next_ref[part, :] = (hidden_ref[part, :].astype(F32) + update).astype(BF16)
        hidden_ref[...] = next_ref[...]

    start = pl.multiple_of(half_ref[0] * own, own)
    key = jnp.dot(
        hidden_ref[...], read_ref[:, channels:], preferred_element_type=F32
    ).astype(BF16)
    query = jnp.dot(
        hidden_ref[pl.ds(start, own), :], read_ref[:, :channels], preferred_element_type=F32
    ).astype(BF16)
    lane = lax.broadcasted_iota(jnp.int32, (64, 128), 1)
    force_ref[...] = jnp.zeros_like(force_ref)
    for part in range(own // 128):
        columns = []
        for piece in range(2):
            first = 128 * part + 64 * piece
            here = pl.ds(start + first, 64)
            pull = lax.dot_general(
                query[first : first + 64],
                key,
                (((1,), (1,)), ((), ())),
                preferred_element_type=F32,
            ) * (pull_ref[here, :] * (1.0 / channels))
            column = jnp.zeros((64, 128), F32)
            for axis in range(3):
                offset = pos_ref[axis : axis + 1, :] - place_ref[here, axis : axis + 1]
                total = jnp.sum(pull * offset, axis=1, keepdims=True)
                column = jnp.where(lane == axis, total, column)
            columns.append(column)
        turned = jnp.transpose(jnp.concatenate(columns, axis=0))[0:8]
        for a in range(128 // share):
            force_ref[128 // share * part + a, :, 0:share] = turned[:, share * a : share * (a + 1)]


def pair_kernel(tiles_ref, own_ref, low_ref, high_ref, force_ref, window_ref, place_ref):
    tiles, listed = tiles_ref.shape
    for which, ref in enumerate((low_ref, own_ref, high_ref)):
        for t in range(tiles):
            window_ref[which * tiles + t, 0:4, :] = ref[:, TILE * t : TILE * (t + 1)]
    for t in range(tiles):
        place_ref[TILE * t : TILE * (t + 1), 0:4] = jnp.transpose(
            own_ref[:, TILE * t : TILE * (t + 1)]
        )
    group = 32
    lane = lax.broadcasted_iota(jnp.int32, (group, 128), 1)

    def one_tile(t, carry):
        near = [tiles_ref[t, c] for c in range(listed)]
        columns = []
        for part in range(TILE // group):
            here = pl.ds(pl.multiple_of(t * TILE + part * group, group), group)
            mine = [place_ref[here, axis : axis + 1] for axis in range(4)]
            sums = [jnp.zeros((group, 128), F32) for _ in range(3)]
            for c in range(listed):
                offsets = [mine[axis] - window_ref[near[c], axis : axis + 1, :] for axis in range(3)]
                squared = SOFTEN
                for offset in offsets:
                    squared = offset * offset + squared
                inverse = lax.rsqrt(squared)
                strength = window_ref[near[c], 3:4, :] * inverse * (inverse * inverse)
                sums = [total + strength * offset for total, offset in zip(sums, offsets)]
            column = jnp.zeros((group, 128), F32)
            for axis in range(3):
                total = jnp.sum(sums[axis], axis=1, keepdims=True) * (COULOMB * mine[3])
                column = jnp.where(lane == axis, total, column)
            columns.append(column)
        turned = jnp.transpose(jnp.concatenate(columns, axis=0))
        force_ref[:, pl.ds(pl.multiple_of(t * TILE, TILE), TILE)] = turned[0:3]
        return carry

    lax.fori_loop(0, tiles, one_tile, 0)


def vmem(count):
    return [pl.BlockSpec(memory_space=pltpu.VMEM)] * count


def on_device(
    mm_positions,
    mm_charge,
    mm_tiles,
    ml_feat,
    ml_positions,
    ml_neighbours,
    msg_weight,
    radial_weight,
    out_weight,
    read_weight,
):
    patches, share, channels = ml_feat.shape
    atom_count = mm_positions.shape[1]
    tile_count, listed = mm_tiles.shape
    members = lax.axis_size("ml")
    size = members * share
    own = size // HALVES
    neighbours = ml_neighbours.shape[1]
    basis_count = radial_weight.shape[1]
    limit = 48 * 1024 * 1024

    send, atoms = pl.pallas_call(
        pack_kernel,
        out_shape=(
            jax.ShapeDtypeStruct((members, share + 16, channels), BF16),
            jax.ShapeDtypeStruct((4, atom_count), F32),
        ),
        in_specs=vmem(5),
        out_specs=tuple(vmem(2)),
        scratch_shapes=[pltpu.VMEM((patches, 16, 128), F32)],
        cost_estimate=pl.CostEstimate(flops=1000, bytes_accessed=400000, transcendentals=0),
    )(ml_feat, ml_positions, ml_neighbours, mm_positions, mm_charge.reshape(1, atom_count))
    recv = lax.all_to_all(send, "ml", split_axis=0, concat_axis=0, tiled=True)

    devices = lax.axis_size(("dom", "ml"))
    forward = [(i, (i + 1) % devices) for i in range(devices)]
    backward = [(b, a) for a, b in forward]
    low = lax.ppermute(atoms, ("dom", "ml"), forward)
    high = lax.ppermute(atoms, ("dom", "ml"), backward)

    half = (lax.axis_index("ml") // patches).astype(jnp.int32).reshape(1)
    forces = pl.pallas_call(
        patch_kernel,
        out_shape=jax.ShapeDtypeStruct((own // share, 8, 128), F32),
        in_specs=[pl.BlockSpec(memory_space=pltpu.SMEM)] + vmem(5),
        out_specs=vmem(1)[0],
        scratch_shapes=[
            pltpu.VMEM((size, channels), BF16),
            pltpu.VMEM((8, size), F32),
            pltpu.VMEM((size, 8), F32),
            pltpu.VMEM((neighbours, size), jnp.int32),
            pltpu.VMEM((neighbours, size), jnp.int32),
            pltpu.VMEM((size, 128), jnp.int32),
            pltpu.VMEM((basis_count, size, size), BF16),
            pltpu.VMEM((size, size), F32),
            pltpu.VMEM((size, channels), BF16),
        ],
        compiler_params=pltpu.CompilerParams(vmem_limit_bytes=limit),
        cost_estimate=pl.CostEstimate(
            flops=5 * 10**9, bytes_accessed=1000000, transcendentals=10**6
        ),
    )(half, recv, msg_weight, radial_weight, out_weight, read_weight)
    groups = [[h * patches + p for p in range(patches)] for h in range(HALVES)]
    returned = lax.all_to_all(
        forces, "ml", split_axis=0, concat_axis=0, tiled=True, axis_index_groups=groups
    )
    ml_force = returned[:, :3, :share]

    mm_force = pl.pallas_call(
        pair_kernel,
        out_shape=jax.ShapeDtypeStruct((3, atom_count), F32),
        in_specs=[pl.BlockSpec(memory_space=pltpu.SMEM)] + vmem(3),
        out_specs=vmem(1)[0],
        scratch_shapes=[
            pltpu.VMEM((3 * tile_count, 8, TILE), F32),
            pltpu.VMEM((atom_count, 8), F32),
        ],
        compiler_params=pltpu.CompilerParams(vmem_limit_bytes=limit),
        cost_estimate=pl.CostEstimate(
            flops=4 * 10**9, bytes_accessed=200000, transcendentals=10**6
        ),
    )(mm_tiles, atoms, low, high)
    return (mm_force, ml_force)


def solution(mesh):
    in_specs = (
        P(None, ("dom", "ml")),
        P(("dom", "ml")),
        P(("dom", "ml"), None),
        P("dom", "ml", None),
        P("dom", None, "ml"),
        P("dom", None, "ml"),
        P(),
        P(),
        P(),
        P(),
    )
    out_specs = (P(None, ("dom", "ml")), P("dom", None, "ml"))
    return jax.shard_map(
        on_device, mesh=mesh, in_specs=in_specs, out_specs=out_specs, check_vma=False
    )
```

time: 729 us -> 48.8 us (0.07)
  local copies, waits for them, and re-layouts: 473 us -> 3.36 us
  waiting for transfers between devices: 89.8 us -> 0.01 us
  blocking collectives: 54.7 us -> 0 us
  matrix products: 40.6 us -> 0 us
  other arithmetic: 32.4 us -> 0 us
  Pallas kernels: 0 us -> 25.5 us
  between operations: 14.1 us -> 0.71 us
    gather x71 -> x0, local copies, waits for them, and re-layouts: 408 us -> none  [the longest x4 243 us: slot_forces(): table_part[:, index_part]]
    all_gather x3 -> x0, waiting for transfers between devices: 82.8 us -> none  [the longest x2 44.7 us: slot_forces(): sender_feat = lax.all_gather(mixed_feat, 'ml', axis=1, tiled=True)]
    squeeze x65 -> x0, local copies, waits for them, and re-layouts: 44.3 us -> none  [the longest x48 44.1 us: slot_forces(): message = lax.map(slot_message, (sender_feat, neighbours, radial_basis))]
    all_gather x1 -> x0, blocking collectives: 43.4 us -> none  [on_device(): all_positions = lax.all_gather(own_positions, 'ml', axis=2, tiled=True)]
    dot_general x52 -> x0, matrix products: 40.6 us -> none  [the longest x32 33 us: slot_message(): jnp.einsum('nkq,nc->kqc', basis_part, radial_map, precision=lax.Precision...]
    pallas_call x0 -> x3, Pallas kernels: none -> 25.5 us  [the longest x1 13.9 us: on_device(): pl.pallas_call(pair_kernel, out_shape=jax.ShapeDtypeStruct((3, atom_count...]
    reduce_sum x51 -> x0, other arithmetic: 23.1 us -> none  [the longest x16 13.3 us: slot_pull(): return jnp.sum(strength[None] * offset_part, axis=1)]
    all_to_all x1 -> x0, blocking collectives: 11.3 us -> none  [on_device(): lax.all_to_all(feat_sent, 'dom', split_axis=0, concat_axis=0, tiled=True)]
  transfers between devices with their start and end apart: 7 -> 4, of which waited for: 4 -> 0; matrix products, arithmetic and copies ran while one was open for 39% -> 0% of each run, Pallas kernels for 0% -> 50%
where the time goes in v1:
time: 48.8 us; the launch traced here: 48 us
  Pallas kernels  25.5 us (52%)
  starting transfers between devices  18.3 us (38%)
  local copies, waits for them, and re-layouts  3.36 us (7%)
  between operations  0.71 us (1%)
    pallas_call x1, Pallas kernels, on_device(): pl.pallas_call(pair_kernel, out_shape=jax.ShapeDtypeStruct((3, atom_count...  13.9 us
    pallas_call x1, Pallas kernels, on_device(): pl.pallas_call(patch_kernel, out_shape=jax.ShapeDtypeStruct((own // share...  9.9 us
    all_to_all x1, starting transfers between devices, on_device(): recv = lax.all_to_all(send, 'ml', split_axis=0, concat_axis=0, tiled=True)  7.26 us
    ppermute x1, starting transfers between devices, on_device(): high = lax.ppermute(atoms, ('dom', 'ml'), backward)  5.76 us
    unnamed x15, local copies, waits for them, and re-layouts  3.36 us
    all_to_all x1, starting transfers between devices, on_device(): lax.all_to_all(forces, 'ml', split_axis=0, concat_axis=0, tiled=True, axi...  3.32 us
    ppermute x1, starting transfers between devices, on_device(): low = lax.ppermute(atoms, ('dom', 'ml'), forward)  1.99 us
    pallas_call x1, Pallas kernels, on_device(): pl.pallas_call(pack_kernel, out_shape=(jax.ShapeDtypeStruct((members, sha...  1.77 us
  transfers between devices with their start and end apart: 4, of which 0 were waited for; matrix products, arithmetic and copies ran while one was open for 0% of the time, Pallas kernels for 50%

profile of v1, /device:TPU:0, one launch (start us, length us, event | category | flops | bytes accessed | tf_op | source)
XLA Modules:
  0.0 48.0 jit_solution(122479274489583703)
XLA Ops:
  0.6 1.3 %copy.12.pos_ref = f32[8,3,32]{2,1,0:T(4,128)} copy(f32[8,3,32]{2,0,1:T(8,128)} %param.14) | data formatting | bytes 6144 | tf_op args[4]
  1.9 1.8 %shard_map.113 = (bf16[16,48,128]{2,1,0:T(8,128)(2,1)}, f32[4,2048]{1,0:T(4,128)}) custom-call(bf16[8,32,128]{2,1,0:T(8,128)(2,1)} %feat_ref.1, f32[8,3,32]{2,1,0:T(4,128)} %copy.12.pos_ref, s32[8,32,32]{2,1,0:T(8,128)} %nb_ref.1, f32[3,2048]{1,0:T(4,128)} %mm_pos_ref.1, f32[1,2048]{1,0:T(1,128)} %bitcast.2), custom_call_target="tpu_custom_call" | custom-call | flops 1000 | bytes 400000 | tf_op jit(solution)/shard_map/pallas_call | solution.py:245
  3.7 0.0 copy-start.3
  3.7 0.0 copy-start
  3.7 0.0 copy-start.1
  3.7 0.0 copy-start.2
  3.7 7.3 %all-to-all-start = ((bf16[16,48,128]{2,1,0:T(8,128)(2,1)}), bf16[16,48,128]{2,1,0:T(8,128)(2,1)S(1)}, u32[]{:S(2)}, u32[]{:S(2)}) async-start(bf16[16,48,128]{2,1,0:T(8,128)(2,1)} %get-tuple-element.5), calls=%async_computation | async-start | bytes 393216 | tf_op jit(solution)/shard_map/all_to_all | solution.py:256
  11.0 0.0 copy-done.3
  11.0 2.0 %collective-permute-start = (f32[4,2048]{1,0:T(4,128)S(1)}, f32[4,2048]{1,0:T(4,128)S(1)}, u32[]{:S(2)}, u32[]{:S(2)}) collective-permute-start(f32[4,2048]{1,0:T(4,128)S(1)} %copy-done.3), channel_id=1, source_target_pairs={{0,1},{1,2},{2,3},{3,4},{4,5},{5,6},{6,7},{7,8},{8,9},{9,10},{10,1... | collective-permute-start | bytes 98312 | tf_op jit(solution)/shard_map/ppermute | solution.py:261
  13.0 5.8 %collective-permute-start.1 = (f32[4,2048]{1,0:T(4,128)S(1)}, f32[4,2048]{1,0:T(4,128)S(1)}, u32[]{:S(2)}, u32[]{:S(2)}) collective-permute-start(f32[4,2048]{1,0:T(4,128)S(1)} %copy-done.3), channel_id=1, source_target_pairs={{1,0},{2,1},{3,2},{4,3},{5,4},{6,5},{7,6},{8,7},{9,8},{10,9},{11,1... | collective-permute-start | bytes 98312 | tf_op jit(solution)/shard_map/ppermute | solution.py:262
  18.8 0.0 copy-start.5
  18.8 0.7 %copy-done.5 = s32[16,8]{0,1:T(8,128)S(1)} copy-done((s32[16,8]{0,1:T(8,128)S(1)}, s32[16,8]{0,1:T(8,128)}, u32[]{:S(2)}) %copy-start.5) | copy-done | bytes 536
  19.5 0.1 copy.13.tiles_ref
  19.5 0.0 copy-start.4
  19.5 0.0 all-to-all-done.recv_ref
  19.5 0.0 copy-done
  19.5 0.0 copy-done.1
  19.5 0.0 copy-done.2
  19.6 0.7 %copy-done.4 = f32[2,8,128]{2,1,0:T(8,128)S(1)} copy-done((f32[2,8,128]{2,1,0:T(8,128)S(1)}, f32[2,8,128]{2,1,0:T(8,128)}, u32[]{:S(2)}) %copy-start.4) | copy-done | bytes 8216
  20.2 9.9 %shard_map.115 = f32[8,8,128]{2,1,0:T(8,128)} custom-call(s32[1]{0:T(128)} %bitcast.1.half_ref, bf16[16,48,128]{2,1,0:T(8,128)(2,1)S(1)} %all-to-all-done.recv_ref, bf16[2,128,128]{2,1,0:T(8,128)(2,1)S(1)} %copy-done, f32[2,8,128]{2,1,0:T(8,128)S(1)} %copy-done.4, bf16[2,128,128]{2,1,0:T(8,128)(2,1)S(1)} %copy-done.1, bf16[128,256]{1,0:T(8,128)(2,1)S(1)} %copy-done.2), custom_call_target="tpu_custom_call" | custom-call | flops 5000000000 | bytes 1000000 | tf_op jit(solution)/shard_map/pallas_call | solution.py:265
  30.1 3.3 %all-to-all-start.1 = ((f32[8,8,128]{2,1,0:T(8,128)}), f32[8,8,128]{2,1,0:T(8,128)S(1)}, u32[]{:S(2)}, u32[]{:S(2)}) async-start(f32[8,8,128]{2,1,0:T(8,128)} %shard_map.115), calls=%async_computation.1 | async-start | bytes 65536 | tf_op jit(solution)/shard_map/all_to_all | solution.py:287
  33.5 0.0 collective-permute-done.low_ref
  33.5 0.0 collective-permute-done.1.high_ref
  33.5 13.9 %shard_map.114 = f32[3,2048]{1,0:T(4,128)} custom-call(s32[16,8]{1,0:T(8,128)S(1)} %copy.13.tiles_ref, f32[4,2048]{1,0:T(4,128)S(1)} %copy-done.3, f32[4,2048]{1,0:T(4,128)S(1)} %collective-permute-done.low_ref, f32[4,2048]{1,0:T(4,128)S(1)} %collective-permute-done.1.high_ref), custom_call_target="tpu_custom_call" | custom-call | flops 4000000000 | bytes 200000 | tf_op jit(solution)/shard_map/pallas_call | solution.py:292
  47.3 0.0 all-to-all-done.1
  47.4 0.6 %copy.14 = f32[8,3,32]{2,0,1:T(8,128)} copy(f32[8,3,32]{2,1,0:T(4,128)S(1)} %slice.4) | data formatting | bytes 6144
  (1 shorter events, 0.0 us)
Async XLA Ops:
  3.7 7.3 %copy-start.3 = (f32[4,2048]{1,0:T(4,128)S(1)}, f32[4,2048]{1,0:T(4,128)}, u32[]{:S(2)}) copy-start(f32[4,2048]{1,0:T(4,128)} %get-tuple-element.4.own_ref) | copy-start | bytes 98308
  3.7 15.8 %copy-start = (bf16[2,128,128]{2,1,0:T(8,128)(2,1)S(1)}, bf16[2,128,128]{2,1,0:T(8,128)(2,1)}, u32[]{:S(2)}) copy-start(bf16[2,128,128]{2,1,0:T(8,128)(2,1)} %msg_ref.1) | copy-start | bytes 196612
  3.7 15.8 %copy-start.1 = (bf16[2,128,128]{2,1,0:T(8,128)(2,1)S(1)}, bf16[2,128,128]{2,1,0:T(8,128)(2,1)}, u32[]{:S(2)}) copy-start(bf16[2,128,128]{2,1,0:T(8,128)(2,1)} %out_w_ref.1) | copy-start | bytes 196612
  3.7 15.8 %copy-start.2 = (bf16[128,256]{1,0:T(8,128)(2,1)S(1)}, bf16[128,256]{1,0:T(8,128)(2,1)}, u32[]{:S(2)}) copy-start(bf16[128,256]{1,0:T(8,128)(2,1)} %read_ref.1) | copy-start | bytes 196612
  3.7 15.8 %all-to-all-start = ((bf16[16,48,128]{2,1,0:T(8,128)(2,1)}), bf16[16,48,128]{2,1,0:T(8,128)(2,1)S(1)}, u32[]{:S(2)}, u32[]{:S(2)}) async-start(bf16[16,48,128]{2,1,0:T(8,128)(2,1)} %get-tuple-element.5), calls=%async_computation | async-start | bytes 393216 | tf_op jit(solution)/shard_map/all_to_all | solution.py:256
  11.0 22.5 %collective-permute-start = (f32[4,2048]{1,0:T(4,128)S(1)}, f32[4,2048]{1,0:T(4,128)S(1)}, u32[]{:S(2)}, u32[]{:S(2)}) collective-permute-start(f32[4,2048]{1,0:T(4,128)S(1)} %copy-done.3), channel_id=1, source_target_pairs={{0,1},{1,2},{2,3},{3,4},{4,5},{5,6},{6,7},{7,8},{8,9},{9,10},{10,1... | collective-permute-start | bytes 98312 | tf_op jit(solution)/shard_map/ppermute | solution.py:261
  13.0 20.5 %collective-permute-start.1 = (f32[4,2048]{1,0:T(4,128)S(1)}, f32[4,2048]{1,0:T(4,128)S(1)}, u32[]{:S(2)}, u32[]{:S(2)}) collective-permute-start(f32[4,2048]{1,0:T(4,128)S(1)} %copy-done.3), channel_id=1, source_target_pairs={{1,0},{2,1},{3,2},{4,3},{5,4},{6,5},{7,6},{8,7},{9,8},{10,9},{11,1... | collective-permute-start | bytes 98312 | tf_op jit(solution)/shard_map/ppermute | solution.py:262
  18.8 0.7 %copy-start.5 = (s32[16,8]{0,1:T(8,128)S(1)}, s32[16,8]{0,1:T(8,128)}, u32[]{:S(2)}) copy-start(s32[16,8]{0,1:T(8,128)} %param.12) | copy-start | bytes 1540
  19.5 0.7 %copy-start.4 = (f32[2,8,128]{2,1,0:T(8,128)S(1)}, f32[2,8,128]{2,1,0:T(8,128)}, u32[]{:S(2)}) copy-start(f32[2,8,128]{2,1,0:T(8,128)} %radial_ref.1) | copy-start | bytes 24580
  30.1 17.2 %all-to-all-start.1 = ((f32[8,8,128]{2,1,0:T(8,128)}), f32[8,8,128]{2,1,0:T(8,128)S(1)}, u32[]{:S(2)}, u32[]{:S(2)}) async-start(f32[8,8,128]{2,1,0:T(8,128)} %shard_map.115), calls=%async_computation.1 | async-start | bytes 65536 | tf_op jit(solution)/shard_map/all_to_all | solution.py:287

commit v2 on v1

v2 whole, which is shorter than its diff:
```python
import math

import jax
import jax.numpy as jnp
from jax import lax
from jax.experimental import pallas as pl
from jax.experimental.pallas import tpu as pltpu
from jax.sharding import PartitionSpec as P

TILE = 128
RADIUS = 6.0
SOFTEN = 1.0
COULOMB = 0.5
HALVES = 2

COSINE = (
    0.9999999991255941,
    -0.23370050635000697,
    0.019968606683524803,
    -0.0008935362638784474,
    2.3601070666008123e-05,
)

F32 = jnp.float32
BF16 = jnp.bfloat16


def split(value):
    high = value.astype(BF16).astype(F32)
    rest = value - high
    middle = rest.astype(BF16).astype(F32)
    return high, middle, rest - middle


LEFT = (0, 0, 1, 1, 0, 2)
RIGHT = (0, 1, 0, 1, 2, 0)


def left_rows(rows_ref, pieces, norm):
    for g, which in enumerate(LEFT):
        rows_ref[4 * g : 4 * g + 4, :] = pieces[which]
    for g, value in enumerate(split(norm + SOFTEN)):
        rows_ref[24 + g : 25 + g, :] = value
    rows_ref[27:30, :] = jnp.ones((3, norm.shape[1]), F32)
    rows_ref[30:32, :] = jnp.zeros((2, norm.shape[1]), F32)


def right_rows(rows_ref, pieces, norm):
    for g, which in enumerate(RIGHT):
        rows_ref[4 * g : 4 * g + 4, :] = pieces[which] * -2.0
    rows_ref[24:27, :] = jnp.ones((3, norm.shape[1]), F32)
    for g, value in enumerate(split(norm)):
        rows_ref[27 + g : 28 + g, :] = value
    rows_ref[30:32, :] = jnp.zeros((2, norm.shape[1]), F32)


def norm_of(place):
    return place[0:1] * place[0:1] + place[1:2] * place[1:2] + place[2:3] * place[2:3]


def pack_kernel(feat_ref, pos_ref, nb_ref, mm_pos_ref, mm_charge_ref, send_ref, atoms_ref, geo_ref):
    patches, atoms, _ = feat_ref.shape
    geo_ref[...] = jnp.zeros_like(geo_ref)
    high, middle, low = split(pos_ref[...])
    for p in range(patches):
        numbers = (nb_ref[p] - 256).astype(F32)
        geo_ref[p, 0:16, 0:32] = numbers[0:16]
        geo_ref[p, 0:16, 32:64] = numbers[16:32]
        for axis in range(3):
            geo_ref[p, axis : axis + 1, 64:96] = high[axis, p : p + 1]
            geo_ref[p, axis : axis + 1, 96:128] = middle[axis, p : p + 1]
            geo_ref[p, axis + 8 : axis + 9, 64:96] = low[axis, p : p + 1]
        block = geo_ref[p].astype(BF16)
        for half in range(HALVES):
            send_ref[half * patches + p, 0:atoms, :] = feat_ref[p]
            send_ref[half * patches + p, atoms : atoms + 16, :] = block
    atoms_ref[0:3, :] = mm_pos_ref[...]
    atoms_ref[3:4, :] = mm_charge_ref[...]


def patch_kernel(
    half_ref,
    recv_ref,
    msg_ref,
    radial_ref,
    out_w_ref,
    read_ref,
    force_ref,
    hidden_ref,
    pos_ref,
    rows_ref,
    near_ref,
    mine_ref,
    side_ref,
    low_ref,
    unit_ref,
    count_ref,
    square_ref,
    basis_ref,
    pull_ref,
    active_ref,
):
    sources = recv_ref.shape[0]
    share = recv_ref.shape[1] - 16
    size = sources * share
    own = size // HALVES
    neighbours = low_ref.shape[0]
    basis_count = radial_ref.shape[1]
    layers = msg_ref.shape[0]
    channels = recv_ref.shape[2]
    blocks = basis_ref.shape[0]
    height = size // blocks
    tiles = size // 128

    for m in range(sources):
        hidden_ref[share * m : share * (m + 1), :] = recv_ref[m, 0:share, :]
        geo = recv_ref[m, share : share + 16, :].astype(F32)
        lanes = slice(share * m, share * (m + 1))
        pos_ref[:, lanes] = (geo[0:8, 64:96] + geo[0:8, 96:128]) + geo[8:16, 64:96]
        low_ref[0:16, lanes] = geo[:, 0:32].astype(jnp.int32) + 256
        low_ref[16:32, lanes] = geo[:, 32:64].astype(jnp.int32) + 256

    def mix(layer):
        return jnp.dot(hidden_ref[...], msg_ref[layer], preferred_element_type=F32).astype(BF16)

    mixed = mix(0)

    place = pos_ref[0:4, :]
    pieces = split(place)
    norm = norm_of(place)
    right_rows(rows_ref, pieces, norm)
    near_ref[...] = rows_ref[...].astype(BF16)
    left_rows(rows_ref, pieces, norm)
    for b in range(tiles):
        at = slice(128 * b, 128 * (b + 1))
        mine_ref[at, :] = jnp.transpose(rows_ref[:, at]).astype(BF16)
    for g, value in enumerate(pieces):
        rows_ref[4 * g : 4 * g + 4, :] = value
    rows_ref[3:4, :] = jnp.ones((1, size), F32)
    rows_ref[12:16, :] = jnp.zeros((4, size), F32)
    side_ref[...] = rows_ref[0:16, :].astype(BF16)
    for b in range(tiles):
        at = slice(128 * b, 128 * (b + 1))
        square_ref[at, :] = jnp.dot(mine_ref[at, :], near_ref[...], preferred_element_type=F32)

    index = low_ref[...]
    low_ref[...] = index & 127
    unit_ref[...] = jnp.int32(1) << ((index >> 7) << 3)
    rows = lax.broadcasted_iota(jnp.int32, (128, 128), 0)

    def count(b):
        lanes = slice(128 * b, 128 * (b + 1))
        total = jnp.zeros((128, 128), jnp.int32)
        for k in range(neighbours):
            total += jnp.where(rows == low_ref[k : k + 1, lanes], unit_ref[k : k + 1, lanes], 0)
        count_ref[lanes, :] = jnp.transpose(total)

    step = 16

    def pairs(b):
        for s in range(height // step):
            here = slice(height * b + step * s, height * b + step * (s + 1))
            packed = count_ref[here, :]
            times = jnp.concatenate(
                [(packed >> (8 * f)) & 255 for f in range(tiles)], axis=1
            ).astype(F32)
            near = jnp.minimum(square_ref[here, :], RADIUS * RADIUS)
            u = near * (1.0 / (RADIUS * RADIUS))
            series = COSINE[4]
            for value in COSINE[3::-1]:
                series = series * u + value
            root = (1.0 - u) * series
            envelope = root * root * times
            pull_ref[here, :] = envelope
            distance = near * lax.rsqrt(near)
            growth = jnp.exp(distance * (4.0 * RADIUS / basis_count))
            basis = jnp.exp(near * -2.0) * envelope
            for n in range(basis_count):
                first = height * n + step * s
                basis_ref[b, first : first + step, :] = basis.astype(BF16)
                if n + 1 < basis_count:
                    basis = basis * growth

    number = lax.broadcasted_iota(jnp.int32, (basis_count, channels), 0).astype(F32)
    center = number * (RADIUS / basis_count)
    scale = jnp.exp(center * center * -2.0) * (1.0 / math.sqrt(neighbours))

    def gather(b, mixed, radial):
        every = jnp.dot(basis_ref[b], mixed, preferred_element_type=F32)
        message = radial[0:1] * every[0:height]
        for n in range(1, basis_count):
            message += radial[n : n + 1] * every[height * n : height * (n + 1)]
        active_ref[height * b : height * (b + 1), :] = jax.nn.silu(message).astype(BF16)

    def update(layer):
        change = jnp.dot(active_ref[...], out_w_ref[layer], preferred_element_type=F32)
        hidden_ref[...] = (hidden_ref[...].astype(F32) + change).astype(BF16)

    radial = radial_ref[0] * scale
    for b in range(blocks):
        if b % (128 // height) == 0:
            count(b // (128 // height))
        pairs(b)
        if b > 0:
            gather(b - 1, mixed, radial)
    gather(blocks - 1, mixed, radial)
    update(0)
    for layer in range(1, layers):
        mixed = mix(layer)
        radial = radial_ref[layer] * scale
        for b in range(blocks):
            gather(b, mixed, radial)
        update(layer)

    start = pl.multiple_of(half_ref[0] * own, own)
    key = jnp.dot(
        hidden_ref[...], read_ref[:, channels:], preferred_element_type=F32
    ).astype(BF16)
    query = jnp.dot(
        hidden_ref[pl.ds(start, own), :], read_ref[:, :channels], preferred_element_type=F32
    ).astype(BF16)
    across = (((1,), (1,)), ((), ()))
    side = side_ref[...]
    force_ref[...] = jnp.zeros_like(force_ref)
    for part in range(own // 128):
        here = pl.ds(start + 128 * part, 128)
        pull = lax.dot_general(
            query[128 * part : 128 * (part + 1)], key, across, preferred_element_type=F32
        ) * (pull_ref[here, :] * (1.0 / channels))
        high = pull.astype(BF16)
        rest = (pull - high.astype(F32)).astype(BF16)
        total = lax.dot_general(high, side, across, preferred_element_type=F32)
        total += lax.dot_general(rest, side, across, preferred_element_type=F32)
        turned = jnp.transpose(total)
        sums = turned[0:4] + turned[4:8] + turned[8:12]
        force = sums[0:3] - pos_ref[0:3, here] * sums[3:4]
        for a in range(128 // share):
            force_ref[128 // share * part + a, 0:3, 0:share] = force[:, share * a : share * (a + 1)]


def pair_kernel(
    tiles_ref,
    own_ref,
    low_ref,
    high_ref,
    force_ref,
    rows_ref,
    value_ref,
    near_ref,
    side_ref,
    mine_ref,
):
    listed, tiles = tiles_ref.shape
    for which, ref in enumerate((low_ref, own_ref, high_ref)):
        place = ref[...]
        pieces = split(place)
        norm = norm_of(place)
        right_rows(rows_ref, pieces, norm)
        charge = place[3:4]
        weighted = jnp.concatenate([place[0:3] * charge, charge], axis=0)
        for g, value in enumerate(split(weighted)):
            value_ref[4 * g : 4 * g + 4, :] = value
        value_ref[12:16, :] = jnp.zeros_like(place)
        for t in range(tiles):
            lanes = slice(TILE * t, TILE * (t + 1))
            near_ref[which * tiles + t] = rows_ref[:, lanes].astype(BF16)
            side_ref[which * tiles + t] = value_ref[:, lanes].astype(BF16)
    place = own_ref[...]
    is_place = lax.broadcasted_iota(jnp.int32, place.shape, 0) < 3
    left_rows(rows_ref, [jnp.where(is_place, piece, 0.0) for piece in split(place)], norm_of(place))
    for t in range(tiles):
        lanes = slice(TILE * t, TILE * (t + 1))
        mine_ref[lanes, :] = jnp.transpose(rows_ref[:, lanes]).astype(BF16)
    across = (((1,), (1,)), ((), ()))
    for t in range(tiles):
        lanes = slice(TILE * t, TILE * (t + 1))
        mine = mine_ref[lanes, :]
        total = jnp.zeros((TILE, 16), F32)
        for c in range(0, listed, 2):
            first, second = tiles_ref[c, t], tiles_ref[c + 1, t]
            squared = jnp.dot(
                mine,
                jnp.concatenate([near_ref[first], near_ref[second]], axis=1),
                preferred_element_type=F32,
            )
            inverse = lax.rsqrt(squared)
            total += lax.dot_general(
                (inverse * inverse * inverse).astype(BF16),
                jnp.concatenate([side_ref[first], side_ref[second]], axis=1),
                across,
                preferred_element_type=F32,
            )
        turned = jnp.transpose(total)
        sums = turned[0:4] + turned[4:8] + turned[8:12]
        place = own_ref[:, lanes]
        force_ref[:, lanes] = (place[0:3] * sums[3:4] - sums[0:3]) * (place[3:4] * COULOMB)


def vmem(count):
    return [pl.BlockSpec(memory_space=pltpu.VMEM)] * count


def on_device(
    mm_positions,
    mm_charge,
    mm_tiles,
    ml_feat,
    ml_positions,
    ml_neighbours,
    msg_weight,
    radial_weight,
    out_weight,
    read_weight,
):
    patches, share, channels = ml_feat.shape
    atom_count = mm_positions.shape[1]
    tile_count, listed = mm_tiles.shape
    members = lax.axis_size("ml")
    size = members * share
    own = size // HALVES
    neighbours = ml_neighbours.shape[1]
    basis_count = radial_weight.shape[1]
    limit = 48 * 1024 * 1024

    send, atoms = pl.pallas_call(
        pack_kernel,
        out_shape=(
            jax.ShapeDtypeStruct((members, share + 16, channels), BF16),
            jax.ShapeDtypeStruct((4, atom_count), F32),
        ),
        in_specs=vmem(5),
        out_specs=tuple(vmem(2)),
        scratch_shapes=[pltpu.VMEM((patches, 16, 128), F32)],
        cost_estimate=pl.CostEstimate(flops=1000, bytes_accessed=400000, transcendentals=0),
    )(
        ml_feat,
        ml_positions.transpose(1, 0, 2),
        ml_neighbours,
        mm_positions,
        mm_charge.reshape(1, atom_count),
    )
    recv = lax.all_to_all(send, "ml", split_axis=0, concat_axis=0, tiled=True)

    devices = lax.axis_size(("dom", "ml"))
    forward = [(i, (i + 1) % devices) for i in range(devices)]
    backward = [(b, a) for a, b in forward]
    low = lax.ppermute(atoms, ("dom", "ml"), forward)
    high = lax.ppermute(atoms, ("dom", "ml"), backward)

    half = (lax.axis_index("ml") // patches).astype(jnp.int32).reshape(1)
    forces = pl.pallas_call(
        patch_kernel,
        out_shape=jax.ShapeDtypeStruct((own // share, 8, 128), F32),
        in_specs=[pl.BlockSpec(memory_space=pltpu.SMEM)] + vmem(5),
        out_specs=vmem(1)[0],
        scratch_shapes=[
            pltpu.VMEM((size, channels), BF16),
            pltpu.VMEM((8, size), F32),
            pltpu.VMEM((32, size), F32),
            pltpu.VMEM((32, size), BF16),
            pltpu.VMEM((size, 32), BF16),
            pltpu.VMEM((16, size), BF16),
            pltpu.VMEM((neighbours, size), jnp.int32),
            pltpu.VMEM((neighbours, size), jnp.int32),
            pltpu.VMEM((size, 128), jnp.int32),
            pltpu.VMEM((size, size), F32),
            pltpu.VMEM((size // 64, basis_count * 64, size), BF16),
            pltpu.VMEM((size, size), F32),
            pltpu.VMEM((size, channels), BF16),
        ],
        compiler_params=pltpu.CompilerParams(vmem_limit_bytes=limit),
        cost_estimate=pl.CostEstimate(
            flops=5 * 10**9, bytes_accessed=1000000, transcendentals=10**6
        ),
    )(half, recv, msg_weight, radial_weight, out_weight, read_weight)
    groups = [[h * patches + p for p in range(patches)] for h in range(HALVES)]
    returned = lax.all_to_all(
        forces, "ml", split_axis=0, concat_axis=0, tiled=True, axis_index_groups=groups
    )
    ml_force = returned[:, :3, :share]

    mm_force = pl.pallas_call(
        pair_kernel,
        out_shape=jax.ShapeDtypeStruct((3, atom_count), F32),
        in_specs=[pl.BlockSpec(memory_space=pltpu.SMEM)] + vmem(3),
        out_specs=vmem(1)[0],
        scratch_shapes=[
            pltpu.VMEM((32, atom_count), F32),
            pltpu.VMEM((16, atom_count), F32),
            pltpu.VMEM((3 * tile_count, 32, TILE), BF16),
            pltpu.VMEM((3 * tile_count, 16, TILE), BF16),
            pltpu.VMEM((atom_count, 32), BF16),
        ],
        compiler_params=pltpu.CompilerParams(vmem_limit_bytes=limit),
        cost_estimate=pl.CostEstimate(
            flops=4 * 10**9, bytes_accessed=200000, transcendentals=10**6
        ),
    )(mm_tiles.T, atoms, low, high)
    return (mm_force, ml_force)


def solution(mesh):
    in_specs = (
        P(None, ("dom", "ml")),
        P(("dom", "ml")),
        P(("dom", "ml"), None),
        P("dom", "ml", None),
        P("dom", None, "ml"),
        P("dom", None, "ml"),
        P(),
        P(),
        P(),
        P(),
    )
    out_specs = (P(None, ("dom", "ml")), P("dom", None, "ml"))
    return jax.shard_map(
        on_device, mesh=mesh, in_specs=in_specs, out_specs=out_specs, check_vma=False
    )
```

time: 48.8 us -> 35 us (0.72)
  Pallas kernels: 25.5 us -> 12.1 us
  waiting for transfers between devices: 0.01 us -> 2.59 us
  local copies, waits for them, and re-layouts: 3.36 us -> 0.83 us
    pallas_call x1, Pallas kernels: 13.9 us -> 4.06 us  [on_device(): pl.pallas_call(pair_kernel, out_shape=jax.ShapeDtypeStruct((3, atom_count...]
    pallas_call x1, Pallas kernels: 9.9 us -> 6.3 us  [on_device(): pl.pallas_call(patch_kernel, out_shape=jax.ShapeDtypeStruct((own // share...]
    unnamed x15 -> x13, local copies, waits for them, and re-layouts: 3.36 us -> 0.82 us
    all_to_all x1, waiting for transfers between devices: 0.01 us -> 2.1 us  [on_device(): lax.all_to_all(forces, 'ml', split_axis=0, concat_axis=0, tiled=True, axi...]
    ppermute x1, starting transfers between devices: 1.99 us -> 0.01 us  [on_device(): low = lax.ppermute(atoms, ('dom', 'ml'), forward)]
    ppermute x1, starting transfers between devices: 5.76 us -> 7.67 us  [on_device(): high = lax.ppermute(atoms, ('dom', 'ml'), backward)]
  transfers between devices with their start and end apart: 4 -> 4, of which waited for: 0 -> 2; matrix products, arithmetic and copies ran while one was open for 0% -> 0% of each run, Pallas kernels for 50% -> 30%
where the time goes in v2:
time: 35 us; the launch traced here: 34.6 us
  starting transfers between devices  18.4 us (53%)
  Pallas kernels  12.1 us (35%)
  waiting for transfers between devices  2.59 us (7%)
  local copies, waits for them, and re-layouts  0.83 us (2%)
  between operations  0.7 us (2%)
    ppermute x1, starting transfers between devices, on_device(): high = lax.ppermute(atoms, ('dom', 'ml'), backward)  7.67 us
    all_to_all x1, starting transfers between devices, on_device(): recv = lax.all_to_all(send, 'ml', split_axis=0, concat_axis=0, tiled=True)  7.26 us
    pallas_call x1, Pallas kernels, on_device(): pl.pallas_call(patch_kernel, out_shape=jax.ShapeDtypeStruct((own // share...  6.3 us
    pallas_call x1, Pallas kernels, on_device(): pl.pallas_call(pair_kernel, out_shape=jax.ShapeDtypeStruct((3, atom_count...  4.06 us
    all_to_all x1, starting transfers between devices, on_device(): lax.all_to_all(forces, 'ml', split_axis=0, concat_axis=0, tiled=True, axi...  3.46 us
    all_to_all x1, waiting for transfers between devices, on_device(): lax.all_to_all(forces, 'ml', split_axis=0, concat_axis=0, tiled=True, axi...  2.1 us
    pallas_call x1, Pallas kernels, on_device(): pl.pallas_call(pack_kernel, out_shape=(jax.ShapeDtypeStruct((members, sha...  1.77 us
    unnamed x13, local copies, waits for them, and re-layouts  0.82 us
  transfers between devices with their start and end apart: 4, of which 2 were waited for; matrix products, arithmetic and copies ran while one was open for 0% of the time, Pallas kernels for 30%

profile of v2, /device:TPU:0, one launch (start us, length us, event | category | flops | bytes accessed | tf_op | source)
XLA Modules:
  0.0 34.6 jit_solution(8823623514593894543)
XLA Ops:
  0.6 1.8 %shard_map.113 = (bf16[16,48,128]{2,1,0:T(8,128)(2,1)}, f32[4,2048]{1,0:T(4,128)}) custom-call(bf16[8,32,128]{2,1,0:T(8,128)(2,1)} %feat_ref.1, f32[3,8,32]{2,1,0:T(8,128)} %bitcast.5, s32[8,32,32]{2,1,0:T(8,128)} %nb_ref.1, f32[3,2048]{1,0:T(4,128)} %mm_pos_ref.1, f32[1,2048]{1,0:T(1,128)} %bitcast.6), custom_call_target="tpu_custom_call" | custom-call | flops 1000 | bytes 400000 | tf_op jit(solution)/shard_map/pallas_call | solution.py:325
  2.4 0.0 copy-start.3
  2.4 0.0 copy-start
  2.4 0.0 copy-start.1
  2.4 0.0 copy-start.2
  2.4 7.3 %all-to-all-start = ((bf16[16,48,128]{2,1,0:T(8,128)(2,1)}), bf16[16,48,128]{2,1,0:T(8,128)(2,1)S(1)}, u32[]{:S(2)}, u32[]{:S(2)}) async-start(bf16[16,48,128]{2,1,0:T(8,128)(2,1)} %get-tuple-element.5), calls=%async_computation | async-start | bytes 393216 | tf_op jit(solution)/shard_map/all_to_all | solution.py:342
  9.7 0.0 copy-done.3
  9.7 7.7 %collective-permute-start.1 = (f32[4,2048]{1,0:T(4,128)S(1)}, f32[4,2048]{1,0:T(4,128)S(1)}, u32[]{:S(2)}, u32[]{:S(2)}) collective-permute-start(f32[4,2048]{1,0:T(4,128)S(1)} %copy-done.3), channel_id=1, source_target_pairs={{1,0},{2,1},{3,2},{4,3},{5,4},{6,5},{7,6},{8,7},{9,8},{10,9},{11,1... | collective-permute-start | bytes 98312 | tf_op jit(solution)/shard_map/ppermute | solution.py:348
  17.4 0.0 collective-permute-start
  17.4 0.0 copy-start.4
  17.4 0.5 %all-to-all-done.recv_ref = bf16[16,48,128]{2,1,0:T(8,128)(2,1)S(1)} async-done(((bf16[16,48,128]{2,1,0:T(8,128)(2,1)}), bf16[16,48,128]{2,1,0:T(8,128)(2,1)S(1)}, u32[]{:S(2)}, u32[]{:S(2)}) %all-to-all-start) | async-done | bytes 196640 | tf_op jit(solution)/shard_map/all_to_all | solution.py:342
  17.9 0.0 copy-done
  17.9 0.0 copy-done.1
  17.9 0.0 copy-done.2
  17.9 0.2 copy-done.4
  18.1 6.3 %shard_map.115 = f32[8,8,128]{2,1,0:T(8,128)} custom-call(s32[1]{0:T(128)} %bitcast.3.half_ref, bf16[16,48,128]{2,1,0:T(8,128)(2,1)S(1)} %all-to-all-done.recv_ref, bf16[2,128,128]{2,1,0:T(8,128)(2,1)S(1)} %copy-done, f32[2,8,128]{2,1,0:T(8,128)S(1)} %copy-done.4, bf16[2,128,128]{2,1,0:T(8,128)(2,1)S(1)} %copy-done.1, bf16[128,256]{1,0:T(8,128)(2,1)S(1)} %copy-done.2), custom_call_target="tpu_custom_call" | custom-call | flops 5000000000 | bytes 1000000 | tf_op jit(solution)/shard_map/pallas_call | solution.py:351
  24.4 0.0 copy-start.5
  24.4 3.5 %all-to-all-start.1 = ((f32[8,8,128]{2,1,0:T(8,128)}), f32[8,8,128]{2,1,0:T(8,128)S(1)}, u32[]{:S(2)}, u32[]{:S(2)}) async-start(f32[8,8,128]{2,1,0:T(8,128)} %shard_map.115), calls=%async_computation.1 | async-start | bytes 65536 | tf_op jit(solution)/shard_map/all_to_all | solution.py:377
  27.8 0.0 collective-permute-done.1.high_ref
  27.9 0.0 collective-permute-done.low_ref
  27.9 0.0 copy-done.5
  27.9 4.1 %shard_map.114 = f32[3,2048]{1,0:T(4,128)} custom-call(s32[8,16]{1,0:T(8,128)S(1)} %bitcast.4, f32[4,2048]{1,0:T(4,128)S(1)} %copy-done.3, f32[4,2048]{1,0:T(4,128)S(1)} %collective-permute-done.low_ref, f32[4,2048]{1,0:T(4,128)S(1)} %collective-permute-done.1.high_ref), custom_call_target="tpu_custom_call" | custom-call | flops 4000000000 | bytes 200000 | tf_op jit(solution)/shard_map/pallas_call | solution.py:382
  31.9 2.1 %all-to-all-done.1 = f32[8,8,128]{2,1,0:T(8,128)S(1)} async-done(((f32[8,8,128]{2,1,0:T(8,128)}), f32[8,8,128]{2,1,0:T(8,128)S(1)}, u32[]{:S(2)}, u32[]{:S(2)}) %all-to-all-start.1) | async-done | bytes 32800 | tf_op jit(solution)/shard_map/all_to_all | solution.py:377
  34.0 0.6 %copy.12 = f32[8,3,32]{2,0,1:T(8,128)} copy(f32[8,3,32]{2,1,0:T(4,128)S(1)} %slice.4) | data formatting | bytes 6144
  (1 shorter events, 0.0 us)
Async XLA Ops:
  2.4 7.3 %copy-start.3 = (f32[4,2048]{1,0:T(4,128)S(1)}, f32[4,2048]{1,0:T(4,128)}, u32[]{:S(2)}) copy-start(f32[4,2048]{1,0:T(4,128)} %get-tuple-element.4.own_ref) | copy-start | bytes 98308
  2.4 15.5 %copy-start = (bf16[2,128,128]{2,1,0:T(8,128)(2,1)S(1)}, bf16[2,128,128]{2,1,0:T(8,128)(2,1)}, u32[]{:S(2)}) copy-start(bf16[2,128,128]{2,1,0:T(8,128)(2,1)} %msg_ref.1) | copy-start | bytes 196612
  2.4 15.5 %copy-start.1 = (bf16[2,128,128]{2,1,0:T(8,128)(2,1)S(1)}, bf16[2,128,128]{2,1,0:T(8,128)(2,1)}, u32[]{:S(2)}) copy-start(bf16[2,128,128]{2,1,0:T(8,128)(2,1)} %out_w_ref.1) | copy-start | bytes 196612
  2.4 15.5 %copy-start.2 = (bf16[128,256]{1,0:T(8,128)(2,1)S(1)}, bf16[128,256]{1,0:T(8,128)(2,1)}, u32[]{:S(2)}) copy-start(bf16[128,256]{1,0:T(8,128)(2,1)} %read_ref.1) | copy-start | bytes 196612
  2.4 15.4 %all-to-all-start = ((bf16[16,48,128]{2,1,0:T(8,128)(2,1)}), bf16[16,48,128]{2,1,0:T(8,128)(2,1)S(1)}, u32[]{:S(2)}, u32[]{:S(2)}) async-start(bf16[16,48,128]{2,1,0:T(8,128)(2,1)} %get-tuple-element.5), calls=%async_computation | async-start | bytes 393216 | tf_op jit(solution)/shard_map/all_to_all | solution.py:342
  9.7 18.1 %collective-permute-start.1 = (f32[4,2048]{1,0:T(4,128)S(1)}, f32[4,2048]{1,0:T(4,128)S(1)}, u32[]{:S(2)}, u32[]{:S(2)}) collective-permute-start(f32[4,2048]{1,0:T(4,128)S(1)} %copy-done.3), channel_id=1, source_target_pairs={{1,0},{2,1},{3,2},{4,3},{5,4},{6,5},{7,6},{8,7},{9,8},{10,9},{11,1... | collective-permute-start | bytes 98312 | tf_op jit(solution)/shard_map/ppermute | solution.py:348
  17.4 10.5 %collective-permute-start = (f32[4,2048]{1,0:T(4,128)S(1)}, f32[4,2048]{1,0:T(4,128)S(1)}, u32[]{:S(2)}, u32[]{:S(2)}) collective-permute-start(f32[4,2048]{1,0:T(4,128)S(1)} %copy-done.3), channel_id=1, source_target_pairs={{0,1},{1,2},{2,3},{3,4},{4,5},{5,6},{6,7},{7,8},{8,9},{9,10},{10,1... | collective-permute-start | bytes 98312 | tf_op jit(solution)/shard_map/ppermute | solution.py:347
  17.4 0.7 %copy-start.4 = (f32[2,8,128]{2,1,0:T(8,128)S(1)}, f32[2,8,128]{2,1,0:T(8,128)}, u32[]{:S(2)}) copy-start(f32[2,8,128]{2,1,0:T(8,128)} %radial_ref.1) | copy-start | bytes 24580
  24.4 3.5 %copy-start.5 = (s32[16,8]{0,1:T(8,128)S(1)}, s32[16,8]{0,1:T(8,128)}, u32[]{:S(2)}) copy-start(s32[16,8]{0,1:T(8,128)} %param.12) | copy-start | bytes 1540
  24.4 9.7 %all-to-all-start.1 = ((f32[8,8,128]{2,1,0:T(8,128)}), f32[8,8,128]{2,1,0:T(8,128)S(1)}, u32[]{:S(2)}, u32[]{:S(2)}) async-start(f32[8,8,128]{2,1,0:T(8,128)} %shard_map.115), calls=%async_computation.1 | async-start | bytes 65536 | tf_op jit(solution)/shard_map/all_to_all | solution.py:377

commit v3 on v2

--- a/solution.py
+++ b/solution.py
@@ -12,6 +12,11 @@
 SOFTEN = 1.0
 COULOMB = 0.5
 HALVES = 2
+
+
+def exchange_order(count):
+    return list(range(count))[::-1]
+
 
 COSINE = (
     0.9999999991255941,
@@ -60,6 +65,8 @@
 
 def pack_kernel(feat_ref, pos_ref, nb_ref, mm_pos_ref, mm_charge_ref, send_ref, atoms_ref, geo_ref):
     patches, atoms, _ = feat_ref.shape
+    members = send_ref.shape[0]
+    holder = exchange_order(patches)
     geo_ref[...] = jnp.zeros_like(geo_ref)
     high, middle, low = split(pos_ref[...])
     for p in range(patches):
@@ -71,9 +78,10 @@
             geo_ref[p, axis : axis + 1, 96:128] = middle[axis, p : p + 1]
             geo_ref[p, axis + 8 : axis + 9, 64:96] = low[axis, p : p + 1]
         block = geo_ref[p].astype(BF16)
-        for half in range(HALVES):
-            send_ref[half * patches + p, 0:atoms, :] = feat_ref[p]
-            send_ref[half * patches + p, atoms : atoms + 16, :] = block
+        for place, member in enumerate(exchange_order(members)):
+            if member % patches == holder[p]:
+                send_ref[place, 0:atoms, :] = feat_ref[p]
+                send_ref[place, atoms : atoms + 16, :] = block
     atoms_ref[0:3, :] = mm_pos_ref[...]
     atoms_ref[3:4, :] = mm_charge_ref[...]
 
@@ -112,9 +120,9 @@
     height = size // blocks
     tiles = size // 128
 
-    for m in range(sources):
-        hidden_ref[share * m : share * (m + 1), :] = recv_ref[m, 0:share, :]
-        geo = recv_ref[m, share : share + 16, :].astype(F32)
+    for place, m in enumerate(exchange_order(sources)):
+        hidden_ref[share * m : share * (m + 1), :] = recv_ref[place, 0:share, :]
+        geo = recv_ref[place, share : share + 16, :].astype(F32)
         lanes = slice(share * m, share * (m + 1))
         pos_ref[:, lanes] = (geo[0:8, 64:96] + geo[0:8, 96:128]) + geo[8:16, 64:96]
         low_ref[0:16, lanes] = geo[:, 0:32].astype(jnp.int32) + 256
@@ -220,6 +228,7 @@
         hidden_ref[pl.ds(start, own), :], read_ref[:, :channels], preferred_element_type=F32
     ).astype(BF16)
     across = (((1,), (1,)), ((), ()))
+    order = exchange_order(own // share)
     side = side_ref[...]
     force_ref[...] = jnp.zeros_like(force_ref)
     for part in range(own // 128):
@@ -235,7 +244,8 @@
         sums = turned[0:4] + turned[4:8] + turned[8:12]
         force = sums[0:3] - pos_ref[0:3, here] * sums[3:4]
         for a in range(128 // share):
-            force_ref[128 // share * part + a, 0:3, 0:share] = force[:, share * a : share * (a + 1)]
+            place = order.index(128 // share * part + a)
+            force_ref[place, 0:3, 0:share] = force[:, share * a : share * (a + 1)]
 
 
 def pair_kernel(
@@ -339,7 +349,14 @@
         mm_positions,
         mm_charge.reshape(1, atom_count),
     )
-    recv = lax.all_to_all(send, "ml", split_axis=0, concat_axis=0, tiled=True)
+    recv = lax.all_to_all(
+        send,
+        "ml",
+        split_axis=0,
+        concat_axis=0,
+        tiled=True,
+        axis_index_groups=[exchange_order(members)],
+    )
 
     devices = lax.axis_size(("dom", "ml"))
     forward = [(i, (i + 1) % devices) for i in range(devices)]
@@ -373,7 +390,7 @@
             flops=5 * 10**9, bytes_accessed=1000000, transcendentals=10**6
         ),
     )(half, recv, msg_weight, radial_weight, out_weight, read_weight)
-    groups = [[h * patches + p for p in range(patches)] for h in range(HALVES)]
+    groups = [[h * patches + p for p in exchange_order(patches)] for h in range(HALVES)]
     returned = lax.all_to_all(
         forces, "ml", split_axis=0, concat_axis=0, tiled=True, axis_index_groups=groups
     )

time: 35 us -> 33.3 us (0.951)
  waiting for transfers between devices: 2.59 us -> 1.29 us
    ppermute x1, starting transfers between devices: 7.67 us -> 3.11 us  [on_device(): high = lax.ppermute(atoms, ('dom', 'ml'), backward)]
    all_to_all x1, starting transfers between devices: 3.46 us -> 6.3 us  [on_device(): lax.all_to_all(forces, 'ml', split_axis=0, concat_axis=0, tiled=True, axi...]
    all_to_all x1, waiting for transfers between devices: 2.1 us -> 0.01 us  [on_device(): lax.all_to_all(forces, 'ml', split_axis=0, concat_axis=0, tiled=True, axi...]
    all_to_all x1, starting transfers between devices: 7.26 us -> 8.84 us  [on_device(): lax.all_to_all(send, 'ml', split_axis=0, concat_axis=0, tiled=True, axis_...]
    all_to_all x1, waiting for transfers between devices: 0.49 us -> 1.28 us  [on_device(): lax.all_to_all(send, 'ml', split_axis=0, concat_axis=0, tiled=True, axis_...]
  transfers between devices with their start and end apart: 4 -> 4, of which waited for: 2 -> 1; matrix products, arithmetic and copies ran while one was open for 0% -> 0% of each run, Pallas kernels for 30% -> 31%
where the time goes in v3:
time: 33.3 us; the launch traced here: 33 us
  starting transfers between devices  18.3 us (55%)
  Pallas kernels  12.1 us (36%)
  waiting for transfers between devices  1.29 us (4%)
  between operations  0.68 us (2%)
  local copies, waits for them, and re-layouts  0.63 us (2%)
    all_to_all x1, starting transfers between devices, on_device(): lax.all_to_all(send, 'ml', split_axis=0, concat_axis=0, tiled=True, axis_...  8.84 us
    all_to_all x1, starting transfers between devices, on_device(): lax.all_to_all(forces, 'ml', split_axis=0, concat_axis=0, tiled=True, axi...  6.3 us
    pallas_call x1, Pallas kernels, on_device(): pl.pallas_call(patch_kernel, out_shape=jax.ShapeDtypeStruct((own // share...  6.28 us
    pallas_call x1, Pallas kernels, on_device(): pl.pallas_call(pair_kernel, out_shape=jax.ShapeDtypeStruct((3, atom_count...  4.06 us
    ppermute x1, starting transfers between devices, on_device(): high = lax.ppermute(atoms, ('dom', 'ml'), backward)  3.11 us
    pallas_call x1, Pallas kernels, on_device(): pl.pallas_call(pack_kernel, out_shape=(jax.ShapeDtypeStruct((members, sha...  1.77 us
    all_to_all x1, waiting for transfers between devices, on_device(): lax.all_to_all(send, 'ml', split_axis=0, concat_axis=0, tiled=True, axis_...  1.28 us
  transfers between devices with their start and end apart: 4, of which 1 were waited for; matrix products, arithmetic and copies ran while one was open for 0% of the time, Pallas kernels for 31%

profile of v3, /device:TPU:0, one launch (start us, length us, event | category | flops | bytes accessed | tf_op | source)
XLA Modules:
  0.0 33.0 jit_solution(2695544740755576319)
XLA Ops:
  0.6 1.8 %shard_map.113 = (bf16[16,48,128]{2,1,0:T(8,128)(2,1)}, f32[4,2048]{1,0:T(4,128)}) custom-call(bf16[8,32,128]{2,1,0:T(8,128)(2,1)} %feat_ref.1, f32[3,8,32]{2,1,0:T(8,128)} %bitcast.5, s32[8,32,32]{2,1,0:T(8,128)} %nb_ref.1, f32[3,2048]{1,0:T(4,128)} %mm_pos_ref.1, f32[1,2048]{1,0:T(1,128)} %bitcast.6), custom_call_target="tpu_custom_call" | custom-call | flops 1000 | bytes 400000 | tf_op jit(solution)/shard_map/pallas_call | solution.py:335
  2.4 0.0 copy-start.3
  2.4 0.0 copy-start
  2.4 0.0 copy-start.1
  2.4 0.0 copy-start.2
  2.4 8.8 %all-to-all-start = ((bf16[16,48,128]{2,1,0:T(8,128)(2,1)}), bf16[16,48,128]{2,1,0:T(8,128)(2,1)S(1)}, u32[]{:S(2)}, u32[]{:S(2)}) async-start(bf16[16,48,128]{2,1,0:T(8,128)(2,1)} %get-tuple-element.5), calls=%async_computation | async-start | bytes 393216 | tf_op jit(solution)/shard_map/all_to_all | solution.py:352
  11.3 0.0 copy-done.3
  11.3 3.1 %collective-permute-start.1 = (f32[4,2048]{1,0:T(4,128)S(1)}, f32[4,2048]{1,0:T(4,128)S(1)}, u32[]{:S(2)}, u32[]{:S(2)}) collective-permute-start(f32[4,2048]{1,0:T(4,128)S(1)} %copy-done.3), channel_id=1, source_target_pairs={{1,0},{2,1},{3,2},{4,3},{5,4},{6,5},{7,6},{8,7},{9,8},{10,9},{11,1... | collective-permute-start | bytes 98312 | tf_op jit(solution)/shard_map/ppermute | solution.py:365
  14.4 0.0 collective-permute-start
  14.4 0.0 copy-start.4
  14.4 1.3 %all-to-all-done.recv_ref = bf16[16,48,128]{2,1,0:T(8,128)(2,1)S(1)} async-done(((bf16[16,48,128]{2,1,0:T(8,128)(2,1)}), bf16[16,48,128]{2,1,0:T(8,128)(2,1)S(1)}, u32[]{:S(2)}, u32[]{:S(2)}) %all-to-all-start) | async-done | bytes 196640 | tf_op jit(solution)/shard_map/all_to_all | solution.py:352
  15.7 0.0 copy-done
  15.7 0.0 copy-done.1
  15.7 0.0 copy-done.2
  15.7 0.0 copy-done.4
  15.7 6.3 %shard_map.115 = f32[8,8,128]{2,1,0:T(8,128)} custom-call(s32[1]{0:T(128)} %bitcast.3.half_ref, bf16[16,48,128]{2,1,0:T(8,128)(2,1)S(1)} %all-to-all-done.recv_ref, bf16[2,128,128]{2,1,0:T(8,128)(2,1)S(1)} %copy-done, f32[2,8,128]{2,1,0:T(8,128)S(1)} %copy-done.4, bf16[2,128,128]{2,1,0:T(8,128)(2,1)S(1)} %copy-done.1, bf16[128,256]{1,0:T(8,128)(2,1)S(1)} %copy-done.2), custom_call_target="tpu_custom_call" | custom-call | flops 5000000000 | bytes 1000000 | tf_op jit(solution)/shard_map/pallas_call | solution.py:368
  22.0 0.0 copy-start.5
  22.0 6.3 %all-to-all-start.1 = ((f32[8,8,128]{2,1,0:T(8,128)}), f32[8,8,128]{2,1,0:T(8,128)S(1)}, u32[]{:S(2)}, u32[]{:S(2)}) async-start(f32[8,8,128]{2,1,0:T(8,128)} %shard_map.115), calls=%async_computation.1 | async-start | bytes 65536 | tf_op jit(solution)/shard_map/all_to_all | solution.py:394
  28.3 0.0 collective-permute-done.1.high_ref
  28.3 0.0 collective-permute-done.low_ref
  28.3 0.0 copy-done.5
  28.3 4.1 %shard_map.114 = f32[3,2048]{1,0:T(4,128)} custom-call(s32[8,16]{1,0:T(8,128)S(1)} %bitcast.4, f32[4,2048]{1,0:T(4,128)S(1)} %copy-done.3, f32[4,2048]{1,0:T(4,128)S(1)} %collective-permute-done.low_ref, f32[4,2048]{1,0:T(4,128)S(1)} %collective-permute-done.1.high_ref), custom_call_target="tpu_custom_call" | custom-call | flops 4000000000 | bytes 200000 | tf_op jit(solution)/shard_map/pallas_call | solution.py:399
  32.4 0.0 all-to-all-done.1
  32.4 0.6 %copy.12 = f32[8,3,32]{2,0,1:T(8,128)} copy(f32[8,3,32]{2,1,0:T(4,128)S(1)} %slice.4) | data formatting | bytes 6144
  (1 shorter events, 0.0 us)
Async XLA Ops:
  2.4 8.9 %copy-start.3 = (f32[4,2048]{1,0:T(4,128)S(1)}, f32[4,2048]{1,0:T(4,128)}, u32[]{:S(2)}) copy-start(f32[4,2048]{1,0:T(4,128)} %get-tuple-element.4.own_ref) | copy-start | bytes 98308
  2.4 13.3 %copy-start = (bf16[2,128,128]{2,1,0:T(8,128)(2,1)S(1)}, bf16[2,128,128]{2,1,0:T(8,128)(2,1)}, u32[]{:S(2)}) copy-start(bf16[2,128,128]{2,1,0:T(8,128)(2,1)} %msg_ref.1) | copy-start | bytes 196612
  2.4 13.3 %copy-start.1 = (bf16[2,128,128]{2,1,0:T(8,128)(2,1)S(1)}, bf16[2,128,128]{2,1,0:T(8,128)(2,1)}, u32[]{:S(2)}) copy-start(bf16[2,128,128]{2,1,0:T(8,128)(2,1)} %out_w_ref.1) | copy-start | bytes 196612
  2.4 13.3 %copy-start.2 = (bf16[128,256]{1,0:T(8,128)(2,1)S(1)}, bf16[128,256]{1,0:T(8,128)(2,1)}, u32[]{:S(2)}) copy-start(bf16[128,256]{1,0:T(8,128)(2,1)} %read_ref.1) | copy-start | bytes 196612
  2.4 13.2 %all-to-all-start = ((bf16[16,48,128]{2,1,0:T(8,128)(2,1)}), bf16[16,48,128]{2,1,0:T(8,128)(2,1)S(1)}, u32[]{:S(2)}, u32[]{:S(2)}) async-start(bf16[16,48,128]{2,1,0:T(8,128)(2,1)} %get-tuple-element.5), calls=%async_computation | async-start | bytes 393216 | tf_op jit(solution)/shard_map/all_to_all | solution.py:352
  11.3 17.0 %collective-permute-start.1 = (f32[4,2048]{1,0:T(4,128)S(1)}, f32[4,2048]{1,0:T(4,128)S(1)}, u32[]{:S(2)}, u32[]{:S(2)}) collective-permute-start(f32[4,2048]{1,0:T(4,128)S(1)} %copy-done.3), channel_id=1, source_target_pairs={{1,0},{2,1},{3,2},{4,3},{5,4},{6,5},{7,6},{8,7},{9,8},{10,9},{11,1... | collective-permute-start | bytes 98312 | tf_op jit(solution)/shard_map/ppermute | solution.py:365
  14.4 13.9 %collective-permute-start = (f32[4,2048]{1,0:T(4,128)S(1)}, f32[4,2048]{1,0:T(4,128)S(1)}, u32[]{:S(2)}, u32[]{:S(2)}) collective-permute-start(f32[4,2048]{1,0:T(4,128)S(1)} %copy-done.3), channel_id=1, source_target_pairs={{0,1},{1,2},{2,3},{3,4},{4,5},{5,6},{6,7},{7,8},{8,9},{9,10},{10,1... | collective-permute-start | bytes 98312 | tf_op jit(solution)/shard_map/ppermute | solution.py:364
  14.4 1.3 %copy-start.4 = (f32[2,8,128]{2,1,0:T(8,128)S(1)}, f32[2,8,128]{2,1,0:T(8,128)}, u32[]{:S(2)}) copy-start(f32[2,8,128]{2,1,0:T(8,128)} %radial_ref.1) | copy-start | bytes 24580
  22.0 6.3 %copy-start.5 = (s32[16,8]{0,1:T(8,128)S(1)}, s32[16,8]{0,1:T(8,128)}, u32[]{:S(2)}) copy-start(s32[16,8]{0,1:T(8,128)} %param.12) | copy-start | bytes 1540
  22.0 10.4 %all-to-all-start.1 = ((f32[8,8,128]{2,1,0:T(8,128)}), f32[8,8,128]{2,1,0:T(8,128)S(1)}, u32[]{:S(2)}, u32[]{:S(2)}) async-start(f32[8,8,128]{2,1,0:T(8,128)} %shard_map.115), calls=%async_computation.1 | async-start | bytes 65536 | tf_op jit(solution)/shard_map/all_to_all | solution.py:394

commit v4 on v3

--- a/solution.py
+++ b/solution.py
@@ -94,6 +94,7 @@
     out_w_ref,
     read_ref,
     force_ref,
+    plain_ref,
     hidden_ref,
     pos_ref,
     rows_ref,
@@ -106,7 +107,6 @@
     square_ref,
     basis_ref,
     pull_ref,
-    active_ref,
 ):
     sources = recv_ref.shape[0]
     share = recv_ref.shape[1] - 16
@@ -116,20 +116,22 @@
     basis_count = radial_ref.shape[1]
     layers = msg_ref.shape[0]
     channels = recv_ref.shape[2]
-    blocks = basis_ref.shape[0]
-    height = size // blocks
     tiles = size // 128
 
     for place, m in enumerate(exchange_order(sources)):
-        hidden_ref[share * m : share * (m + 1), :] = recv_ref[place, 0:share, :]
+        plain_ref[share * m : share * (m + 1), :] = recv_ref[place, 0:share, :]
         geo = recv_ref[place, share : share + 16, :].astype(F32)
         lanes = slice(share * m, share * (m + 1))
         pos_ref[:, lanes] = (geo[0:8, 64:96] + geo[0:8, 96:128]) + geo[8:16, 64:96]
         low_ref[0:16, lanes] = geo[:, 0:32].astype(jnp.int32) + 256
         low_ref[16:32, lanes] = geo[:, 32:64].astype(jnp.int32) + 256
+    hidden_ref[...] = jnp.transpose(plain_ref[...])
+    msg = [jnp.transpose(msg_ref[layer]) for layer in range(layers)]
+    out_w = [jnp.transpose(out_w_ref[layer]) for layer in range(layers)]
+    read = jnp.transpose(read_ref[...])
 
     def mix(layer):
-        return jnp.dot(hidden_ref[...], msg_ref[layer], preferred_element_type=F32).astype(BF16)
+        return jnp.dot(msg[layer], hidden_ref[...], preferred_element_type=F32).astype(BF16)
 
     mixed = mix(0)
 
@@ -147,9 +149,7 @@
     rows_ref[3:4, :] = jnp.ones((1, size), F32)
     rows_ref[12:16, :] = jnp.zeros((4, size), F32)
     side_ref[...] = rows_ref[0:16, :].astype(BF16)
-    for b in range(tiles):
-        at = slice(128 * b, 128 * (b + 1))
-        square_ref[at, :] = jnp.dot(mine_ref[at, :], near_ref[...], preferred_element_type=F32)
+    square_ref[...] = jnp.dot(mine_ref[...], near_ref[...], preferred_element_type=F32)
 
     index = low_ref[...]
     low_ref[...] = index & 127
@@ -161,91 +161,79 @@
         total = jnp.zeros((128, 128), jnp.int32)
         for k in range(neighbours):
             total += jnp.where(rows == low_ref[k : k + 1, lanes], unit_ref[k : k + 1, lanes], 0)
-        count_ref[lanes, :] = jnp.transpose(total)
-
-    step = 16
-
-    def pairs(b):
-        for s in range(height // step):
-            here = slice(height * b + step * s, height * b + step * (s + 1))
-            packed = count_ref[here, :]
-            times = jnp.concatenate(
-                [(packed >> (8 * f)) & 255 for f in range(tiles)], axis=1
-            ).astype(F32)
-            near = jnp.minimum(square_ref[here, :], RADIUS * RADIUS)
-            u = near * (1.0 / (RADIUS * RADIUS))
-            series = COSINE[4]
-            for value in COSINE[3::-1]:
-                series = series * u + value
-            root = (1.0 - u) * series
+        count_ref[:, lanes] = total
+
+    step = 32
+    limit = RADIUS * RADIUS
+    per_basis = 4.0 * RADIUS / basis_count / math.log(2.0)
+    series = [value / limit ** (k + 1) for k, value in enumerate(COSINE)]
+
+    def pairs(lanes):
+        for s in range(size // step):
+            here = slice(step * s, step * (s + 1))
+            f, first = divmod(step * s, 128)
+            times = ((count_ref[first : first + step, lanes] >> (8 * f)) & 255).astype(F32)
+            near = jnp.minimum(square_ref[here, lanes], limit)
+            root = series[-1]
+            for value in series[-2::-1]:
+                root = root * near + value
+            root = (limit - near) * root
             envelope = root * root * times
-            pull_ref[here, :] = envelope
-            distance = near * lax.rsqrt(near)
-            growth = jnp.exp(distance * (4.0 * RADIUS / basis_count))
-            basis = jnp.exp(near * -2.0) * envelope
+            pull_ref[here, lanes] = envelope
+            growth = jnp.exp2(near * lax.rsqrt(near) * per_basis)
+            basis = jnp.exp2(near * (-2.0 / math.log(2.0))) * envelope
             for n in range(basis_count):
-                first = height * n + step * s
-                basis_ref[b, first : first + step, :] = basis.astype(BF16)
+                basis_ref[n, here, lanes] = basis.astype(BF16)
                 if n + 1 < basis_count:
                     basis = basis * growth
 
     number = lax.broadcasted_iota(jnp.int32, (basis_count, channels), 0).astype(F32)
     center = number * (RADIUS / basis_count)
     scale = jnp.exp(center * center * -2.0) * (1.0 / math.sqrt(neighbours))
-
-    def gather(b, mixed, radial):
-        every = jnp.dot(basis_ref[b], mixed, preferred_element_type=F32)
-        message = radial[0:1] * every[0:height]
-        for n in range(1, basis_count):
-            message += radial[n : n + 1] * every[height * n : height * (n + 1)]
-        active_ref[height * b : height * (b + 1), :] = jax.nn.silu(message).astype(BF16)
-
-    def update(layer):
-        change = jnp.dot(active_ref[...], out_w_ref[layer], preferred_element_type=F32)
-        hidden_ref[...] = (hidden_ref[...].astype(F32) + change).astype(BF16)
-
-    radial = radial_ref[0] * scale
-    for b in range(blocks):
-        if b % (128 // height) == 0:
-            count(b // (128 // height))
-        pairs(b)
-        if b > 0:
-            gather(b - 1, mixed, radial)
-    gather(blocks - 1, mixed, radial)
-    update(0)
-    for layer in range(1, layers):
-        mixed = mix(layer)
-        radial = radial_ref[layer] * scale
-        for b in range(blocks):
-            gather(b, mixed, radial)
-        update(layer)
-
-    start = pl.multiple_of(half_ref[0] * own, own)
-    key = jnp.dot(
-        hidden_ref[...], read_ref[:, channels:], preferred_element_type=F32
+    radial = [jnp.transpose(radial_ref[layer] * scale) for layer in range(layers)]
+
+    def advance(layer, lanes, mixed):
+        message = 0.0
+        for n in range(basis_count):
+            message += radial[layer][:, n : n + 1] * jnp.dot(
+                mixed, basis_ref[n, :, lanes], preferred_element_type=F32
+            )
+        active = jax.nn.silu(message).astype(BF16)
+        change = jnp.dot(out_w[layer], active, preferred_element_type=F32)
+        return (hidden_ref[:, lanes].astype(F32) + change).astype(BF16)
+
+    parts = [slice(own * part, own * (part + 1)) for part in range(HALVES)]
+    for part, lanes in enumerate(parts):
+        for b in range(tiles // HALVES):
+            count(tiles // HALVES * part + b)
+        pairs(lanes)
+    for layer in range(layers):
+        if layer > 0:
+            mixed = mix(layer)
+        later = [advance(layer, lanes, mixed) for lanes in parts]
+        for lanes, value in zip(parts, later):
+            hidden_ref[:, lanes] = value
+
+    mine = pl.ds(pl.multiple_of(half_ref[0] * own, own), own)
+    key = jnp.transpose(
+        jnp.dot(read[channels:], hidden_ref[...], preferred_element_type=F32)
     ).astype(BF16)
-    query = jnp.dot(
-        hidden_ref[pl.ds(start, own), :], read_ref[:, :channels], preferred_element_type=F32
-    ).astype(BF16)
-    across = (((1,), (1,)), ((), ()))
-    order = exchange_order(own // share)
+    query = jnp.dot(read[:channels], hidden_ref[:, mine], preferred_element_type=F32).astype(BF16)
     side = side_ref[...]
-    force_ref[...] = jnp.zeros_like(force_ref)
-    for part in range(own // 128):
-        here = pl.ds(start + 128 * part, 128)
-        pull = lax.dot_general(
-            query[128 * part : 128 * (part + 1)], key, across, preferred_element_type=F32
-        ) * (pull_ref[here, :] * (1.0 / channels))
+    total = jnp.zeros((16, own), F32)
+    for here in parts:
+        pull = jnp.dot(key[here], query, preferred_element_type=F32) * (
+            pull_ref[here, mine] * (1.0 / channels)
+        )
         high = pull.astype(BF16)
         rest = (pull - high.astype(F32)).astype(BF16)
-        total = lax.dot_general(high, side, across, preferred_element_type=F32)
-        total += lax.dot_general(rest, side, across, preferred_element_type=F32)
-        turned = jnp.transpose(total)
-        sums = turned[0:4] + turned[4:8] + turned[8:12]
-        force = sums[0:3] - pos_ref[0:3, here] * sums[3:4]
-        for a in range(128 // share):
-            place = order.index(128 // share * part + a)
-            force_ref[place, 0:3, 0:share] = force[:, share * a : share * (a + 1)]
+        total += jnp.dot(side[:, here], high, preferred_element_type=F32)
+        total += jnp.dot(side[:, here], rest, preferred_element_type=F32)
+    sums = total[0:4] + total[4:8] + total[8:12]
+    force = sums[0:3] - pos_ref[0:3, mine] * sums[3:4]
+    force_ref[...] = jnp.zeros_like(force_ref)
+    for place, a in enumerate(exchange_order(own // share)):
+        force_ref[place, 0:3, 0:share] = force[:, share * a : share * (a + 1)]
 
 
 def pair_kernel(
@@ -372,6 +360,7 @@
         out_specs=vmem(1)[0],
         scratch_shapes=[
             pltpu.VMEM((size, channels), BF16),
+            pltpu.VMEM((channels, size), BF16),
             pltpu.VMEM((8, size), F32),
             pltpu.VMEM((32, size), F32),
             pltpu.VMEM((32, size), BF16),
@@ -379,11 +368,10 @@
             pltpu.VMEM((16, size), BF16),
             pltpu.VMEM((neighbours, size), jnp.int32),
             pltpu.VMEM((neighbours, size), jnp.int32),
-            pltpu.VMEM((size, 128), jnp.int32),
+            pltpu.VMEM((128, size), jnp.int32),
             pltpu.VMEM((size, size), F32),
-            pltpu.VMEM((size // 64, basis_count * 64, size), BF16),
+            pltpu.VMEM((basis_count, size, size), BF16),
             pltpu.VMEM((size, size), F32),
-            pltpu.VMEM((size, channels), BF16),
         ],
         compiler_params=pltpu.CompilerParams(vmem_limit_bytes=limit),
         cost_estimate=pl.CostEstimate(

time: 33.3 us -> 32.9 us (0.988)
  Pallas kernels: 12.1 us -> 11.7 us
    pallas_call x1, Pallas kernels: 6.28 us -> 5.84 us  [on_device(): pl.pallas_call(patch_kernel, out_shape=jax.ShapeDtypeStruct((own // share...]
  transfers between devices with their start and end apart: 4 -> 4, of which waited for: 1 -> 1; matrix products, arithmetic and copies ran while one was open for 0% -> 0% of each run, Pallas kernels for 31% -> 30%
where the time goes in v4:
time: 32.9 us; the launch traced here: 32.5 us
  starting transfers between devices  18.2 us (55%)
  Pallas kernels  11.7 us (36%)
  waiting for transfers between devices  1.29 us (4%)
  between operations  0.68 us (2%)
  local copies, waits for them, and re-layouts  0.63 us (2%)
    all_to_all x1, starting transfers between devices, on_device(): lax.all_to_all(send, 'ml', split_axis=0, concat_axis=0, tiled=True, axis_...  8.84 us
    all_to_all x1, starting transfers between devices, on_device(): lax.all_to_all(forces, 'ml', split_axis=0, concat_axis=0, tiled=True, axi...  6.29 us
    pallas_call x1, Pallas kernels, on_device(): pl.pallas_call(patch_kernel, out_shape=jax.ShapeDtypeStruct((own // share...  5.84 us
    pallas_call x1, Pallas kernels, on_device(): pl.pallas_call(pair_kernel, out_shape=jax.ShapeDtypeStruct((3, atom_count...  4.06 us
    ppermute x1, starting transfers between devices, on_device(): high = lax.ppermute(atoms, ('dom', 'ml'), backward)  3.11 us
    pallas_call x1, Pallas kernels, on_device(): pl.pallas_call(pack_kernel, out_shape=(jax.ShapeDtypeStruct((members, sha...  1.77 us
    all_to_all x1, waiting for transfers between devices, on_device(): lax.all_to_all(send, 'ml', split_axis=0, concat_axis=0, tiled=True, axis_...  1.28 us
  transfers between devices with their start and end apart: 4, of which 1 were waited for; matrix products, arithmetic and copies ran while one was open for 0% of the time, Pallas kernels for 30%

profile of v4, /device:TPU:0, one launch (start us, length us, event | category | flops | bytes accessed | tf_op | source)
XLA Modules:
  0.0 32.5 jit_solution(6787409671917848007)
XLA Ops:
  0.6 1.8 %shard_map.113 = (bf16[16,48,128]{2,1,0:T(8,128)(2,1)}, f32[4,2048]{1,0:T(4,128)}) custom-call(bf16[8,32,128]{2,1,0:T(8,128)(2,1)} %feat_ref.1, f32[3,8,32]{2,1,0:T(8,128)} %bitcast.5, s32[8,32,32]{2,1,0:T(8,128)} %nb_ref.1, f32[3,2048]{1,0:T(4,128)} %mm_pos_ref.1, f32[1,2048]{1,0:T(1,128)} %bitcast.6), custom_call_target="tpu_custom_call" | custom-call | flops 1000 | bytes 400000 | tf_op jit(solution)/shard_map/pallas_call | solution.py:323
  2.4 0.0 copy-start.3
  2.4 0.0 copy-start
  2.4 0.0 copy-start.1
  2.4 0.0 copy-start.2
  2.4 8.8 %all-to-all-start = ((bf16[16,48,128]{2,1,0:T(8,128)(2,1)}), bf16[16,48,128]{2,1,0:T(8,128)(2,1)S(1)}, u32[]{:S(2)}, u32[]{:S(2)}) async-start(bf16[16,48,128]{2,1,0:T(8,128)(2,1)} %get-tuple-element.5), calls=%async_computation | async-start | bytes 393216 | tf_op jit(solution)/shard_map/all_to_all | solution.py:340
  11.3 0.0 copy-done.3
  11.3 3.1 %collective-permute-start.1 = (f32[4,2048]{1,0:T(4,128)S(1)}, f32[4,2048]{1,0:T(4,128)S(1)}, u32[]{:S(2)}, u32[]{:S(2)}) collective-permute-start(f32[4,2048]{1,0:T(4,128)S(1)} %copy-done.3), channel_id=1, source_target_pairs={{1,0},{2,1},{3,2},{4,3},{5,4},{6,5},{7,6},{8,7},{9,8},{10,9},{11,1... | collective-permute-start | bytes 98312 | tf_op jit(solution)/shard_map/ppermute | solution.py:353
  14.4 0.0 collective-permute-start
  14.4 0.0 copy-start.4
  14.4 1.3 %all-to-all-done.recv_ref = bf16[16,48,128]{2,1,0:T(8,128)(2,1)S(1)} async-done(((bf16[16,48,128]{2,1,0:T(8,128)(2,1)}), bf16[16,48,128]{2,1,0:T(8,128)(2,1)S(1)}, u32[]{:S(2)}, u32[]{:S(2)}) %all-to-all-start) | async-done | bytes 196640 | tf_op jit(solution)/shard_map/all_to_all | solution.py:340
  15.7 0.0 copy-done
  15.7 0.0 copy-done.1
  15.7 0.0 copy-done.2
  15.7 0.0 copy-done.4
  15.7 5.8 %shard_map.115 = f32[8,8,128]{2,1,0:T(8,128)} custom-call(s32[1]{0:T(128)} %bitcast.3.half_ref, bf16[16,48,128]{2,1,0:T(8,128)(2,1)S(1)} %all-to-all-done.recv_ref, bf16[2,128,128]{2,1,0:T(8,128)(2,1)S(1)} %copy-done, f32[2,8,128]{2,1,0:T(8,128)S(1)} %copy-done.4, bf16[2,128,128]{2,1,0:T(8,128)(2,1)S(1)} %copy-done.1, bf16[128,256]{1,0:T(8,128)(2,1)S(1)} %copy-done.2), custom_call_target="tpu_custom_call" | custom-call | flops 5000000000 | bytes 1000000 | tf_op jit(solution)/shard_map/pallas_call | solution.py:356
  21.5 0.0 copy-start.5
  21.5 6.3 %all-to-all-start.1 = ((f32[8,8,128]{2,1,0:T(8,128)}), f32[8,8,128]{2,1,0:T(8,128)S(1)}, u32[]{:S(2)}, u32[]{:S(2)}) async-start(f32[8,8,128]{2,1,0:T(8,128)} %shard_map.115), calls=%async_computation.1 | async-start | bytes 65536 | tf_op jit(solution)/shard_map/all_to_all | solution.py:382
  27.8 0.0 collective-permute-done.1.high_ref
  27.8 0.0 collective-permute-done.low_ref
  27.8 0.0 copy-done.5
  27.9 4.1 %shard_map.114 = f32[3,2048]{1,0:T(4,128)} custom-call(s32[8,16]{1,0:T(8,128)S(1)} %bitcast.4, f32[4,2048]{1,0:T(4,128)S(1)} %copy-done.3, f32[4,2048]{1,0:T(4,128)S(1)} %collective-permute-done.low_ref, f32[4,2048]{1,0:T(4,128)S(1)} %collective-permute-done.1.high_ref), custom_call_target="tpu_custom_call" | custom-call | flops 4000000000 | bytes 200000 | tf_op jit(solution)/shard_map/pallas_call | solution.py:387
  31.9 0.0 all-to-all-done.1
  31.9 0.6 %copy.12 = f32[8,3,32]{2,0,1:T(8,128)} copy(f32[8,3,32]{2,1,0:T(4,128)S(1)} %slice.4) | data formatting | bytes 6144
  (1 shorter events, 0.0 us)
Async XLA Ops:
  2.4 8.9 %copy-start.3 = (f32[4,2048]{1,0:T(4,128)S(1)}, f32[4,2048]{1,0:T(4,128)}, u32[]{:S(2)}) copy-start(f32[4,2048]{1,0:T(4,128)} %get-tuple-element.4.own_ref) | copy-start | bytes 98308
  2.4 13.3 %copy-start = (bf16[2,128,128]{2,1,0:T(8,128)(2,1)S(1)}, bf16[2,128,128]{2,1,0:T(8,128)(2,1)}, u32[]{:S(2)}) copy-start(bf16[2,128,128]{2,1,0:T(8,128)(2,1)} %msg_ref.1) | copy-start | bytes 196612
  2.4 13.3 %copy-start.1 = (bf16[2,128,128]{2,1,0:T(8,128)(2,1)S(1)}, bf16[2,128,128]{2,1,0:T(8,128)(2,1)}, u32[]{:S(2)}) copy-start(bf16[2,128,128]{2,1,0:T(8,128)(2,1)} %out_w_ref.1) | copy-start | bytes 196612
  2.4 13.3 %copy-start.2 = (bf16[128,256]{1,0:T(8,128)(2,1)S(1)}, bf16[128,256]{1,0:T(8,128)(2,1)}, u32[]{:S(2)}) copy-start(bf16[128,256]{1,0:T(8,128)(2,1)} %read_ref.1) | copy-start | bytes 196612
  2.4 13.2 %all-to-all-start = ((bf16[16,48,128]{2,1,0:T(8,128)(2,1)}), bf16[16,48,128]{2,1,0:T(8,128)(2,1)S(1)}, u32[]{:S(2)}, u32[]{:S(2)}) async-start(bf16[16,48,128]{2,1,0:T(8,128)(2,1)} %get-tuple-element.5), calls=%async_computation | async-start | bytes 393216 | tf_op jit(solution)/shard_map/all_to_all | solution.py:340
  11.3 16.6 %collective-permute-start.1 = (f32[4,2048]{1,0:T(4,128)S(1)}, f32[4,2048]{1,0:T(4,128)S(1)}, u32[]{:S(2)}, u32[]{:S(2)}) collective-permute-start(f32[4,2048]{1,0:T(4,128)S(1)} %copy-done.3), channel_id=1, source_target_pairs={{1,0},{2,1},{3,2},{4,3},{5,4},{6,5},{7,6},{8,7},{9,8},{10,9},{11,1... | collective-permute-start | bytes 98312 | tf_op jit(solution)/shard_map/ppermute | solution.py:353
  14.4 13.5 %collective-permute-start = (f32[4,2048]{1,0:T(4,128)S(1)}, f32[4,2048]{1,0:T(4,128)S(1)}, u32[]{:S(2)}, u32[]{:S(2)}) collective-permute-start(f32[4,2048]{1,0:T(4,128)S(1)} %copy-done.3), channel_id=1, source_target_pairs={{0,1},{1,2},{2,3},{3,4},{4,5},{5,6},{6,7},{7,8},{8,9},{9,10},{10,1... | collective-permute-start | bytes 98312 | tf_op jit(solution)/shard_map/ppermute | solution.py:352
  14.4 1.3 %copy-start.4 = (f32[2,8,128]{2,1,0:T(8,128)S(1)}, f32[2,8,128]{2,1,0:T(8,128)}, u32[]{:S(2)}) copy-start(f32[2,8,128]{2,1,0:T(8,128)} %radial_ref.1) | copy-start | bytes 24580
  21.5 6.3 %copy-start.5 = (s32[16,8]{0,1:T(8,128)S(1)}, s32[16,8]{0,1:T(8,128)}, u32[]{:S(2)}) copy-start(s32[16,8]{0,1:T(8,128)} %param.12) | copy-start | bytes 1540
  21.5 10.4 %all-to-all-start.1 = ((f32[8,8,128]{2,1,0:T(8,128)}), f32[8,8,128]{2,1,0:T(8,128)S(1)}, u32[]{:S(2)}, u32[]{:S(2)}) async-start(f32[8,8,128]{2,1,0:T(8,128)} %shard_map.115), calls=%async_computation.1 | async-start | bytes 65536 | tf_op jit(solution)/shard_map/all_to_all | solution.py:382

commit v5 on v4

--- a/solution.py
+++ b/solution.py
@@ -14,8 +14,12 @@
 HALVES = 2
 
 
+FIRST = {16: 10, 8: 2}
+
+
 def exchange_order(count):
-    return list(range(count))[::-1]
+    first = FIRST.get(count, count - 1)
+    return [first] + [member for member in range(count)[::-1] if member != first]
 
 
 COSINE = (
@@ -63,7 +67,18 @@
     return place[0:1] * place[0:1] + place[1:2] * place[1:2] + place[2:3] * place[2:3]
 
 
-def pack_kernel(feat_ref, pos_ref, nb_ref, mm_pos_ref, mm_charge_ref, send_ref, atoms_ref, geo_ref):
+def pack_kernel(
+    feat_ref,
+    pos_ref,
+    nb_ref,
+    mm_pos_ref,
+    mm_charge_ref,
+    radial_ref,
+    send_ref,
+    atoms_ref,
+    near_radial_ref,
+    geo_ref,
+):
     patches, atoms, _ = feat_ref.shape
     members = send_ref.shape[0]
     holder = exchange_order(patches)
@@ -84,10 +99,10 @@
                 send_ref[place, atoms : atoms + 16, :] = block
     atoms_ref[0:3, :] = mm_pos_ref[...]
     atoms_ref[3:4, :] = mm_charge_ref[...]
+    near_radial_ref[...] = radial_ref[...]
 
 
 def patch_kernel(
-    half_ref,
     recv_ref,
     msg_ref,
     radial_ref,
@@ -214,7 +229,8 @@
         for lanes, value in zip(parts, later):
             hidden_ref[:, lanes] = value
 
-    mine = pl.ds(pl.multiple_of(half_ref[0] * own, own), own)
+    half = lax.axis_index("ml") // (sources // HALVES)
+    mine = pl.ds(pl.multiple_of(half * own, own), own)
     key = jnp.transpose(
         jnp.dot(read[channels:], hidden_ref[...], preferred_element_type=F32)
     ).astype(BF16)
@@ -237,7 +253,7 @@
 
 
 def pair_kernel(
-    tiles_ref,
+    tiles_hbm_ref,
     own_ref,
     low_ref,
     high_ref,
@@ -247,8 +263,12 @@
     near_ref,
     side_ref,
     mine_ref,
+    tiles_ref,
+    tiles_sem,
 ):
     listed, tiles = tiles_ref.shape
+    tiles_copy = pltpu.make_async_copy(tiles_hbm_ref, tiles_ref, tiles_sem)
+    tiles_copy.start()
     for which, ref in enumerate((low_ref, own_ref, high_ref)):
         place = ref[...]
         pieces = split(place)
@@ -270,6 +290,7 @@
         lanes = slice(TILE * t, TILE * (t + 1))
         mine_ref[lanes, :] = jnp.transpose(rows_ref[:, lanes]).astype(BF16)
     across = (((1,), (1,)), ((), ()))
+    tiles_copy.wait()
     for t in range(tiles):
         lanes = slice(TILE * t, TILE * (t + 1))
         mine = mine_ref[lanes, :]
@@ -320,14 +341,15 @@
     basis_count = radial_weight.shape[1]
     limit = 48 * 1024 * 1024
 
-    send, atoms = pl.pallas_call(
+    send, atoms, near_radial = pl.pallas_call(
         pack_kernel,
         out_shape=(
             jax.ShapeDtypeStruct((members, share + 16, channels), BF16),
-            jax.ShapeDtypeStruct((4, atom_count), F32),
+            pltpu.VMEM((4, atom_count), F32),
+            pltpu.VMEM(radial_weight.shape, F32),
         ),
-        in_specs=vmem(5),
-        out_specs=tuple(vmem(2)),
+        in_specs=vmem(6),
+        out_specs=tuple(vmem(3)),
         scratch_shapes=[pltpu.VMEM((patches, 16, 128), F32)],
         cost_estimate=pl.CostEstimate(flops=1000, bytes_accessed=400000, transcendentals=0),
     )(
@@ -336,6 +358,7 @@
         ml_neighbours,
         mm_positions,
         mm_charge.reshape(1, atom_count),
+        radial_weight,
     )
     recv = lax.all_to_all(
         send,
@@ -352,11 +375,10 @@
     low = lax.ppermute(atoms, ("dom", "ml"), forward)
     high = lax.ppermute(atoms, ("dom", "ml"), backward)
 
-    half = (lax.axis_index("ml") // patches).astype(jnp.int32).reshape(1)
     forces = pl.pallas_call(
         patch_kernel,
         out_shape=jax.ShapeDtypeStruct((own // share, 8, 128), F32),
-        in_specs=[pl.BlockSpec(memory_space=pltpu.SMEM)] + vmem(5),
+        in_specs=vmem(5),
         out_specs=vmem(1)[0],
         scratch_shapes=[
             pltpu.VMEM((size, channels), BF16),
@@ -377,7 +399,7 @@
         cost_estimate=pl.CostEstimate(
             flops=5 * 10**9, bytes_accessed=1000000, transcendentals=10**6
         ),
-    )(half, recv, msg_weight, radial_weight, out_weight, read_weight)
+    )(recv, msg_weight, near_radial, out_weight, read_weight)
     groups = [[h * patches + p for p in exchange_order(patches)] for h in range(HALVES)]
     returned = lax.all_to_all(
         forces, "ml", split_axis=0, concat_axis=0, tiled=True, axis_index_groups=groups
@@ -387,7 +409,7 @@
     mm_force = pl.pallas_call(
         pair_kernel,
         out_shape=jax.ShapeDtypeStruct((3, atom_count), F32),
-        in_specs=[pl.BlockSpec(memory_space=pltpu.SMEM)] + vmem(3),
+        in_specs=[pl.BlockSpec(memory_space=pl.ANY)] + vmem(3),
         out_specs=vmem(1)[0],
         scratch_shapes=[
             pltpu.VMEM((32, atom_count), F32),
@@ -395,6 +417,8 @@
             pltpu.VMEM((3 * tile_count, 32, TILE), BF16),
             pltpu.VMEM((3 * tile_count, 16, TILE), BF16),
             pltpu.VMEM((atom_count, 32), BF16),
+            pltpu.SMEM((listed, tile_count), jnp.int32),
+            pltpu.SemaphoreType.DMA,
         ],
         compiler_params=pltpu.CompilerParams(vmem_limit_bytes=limit),
         cost_estimate=pl.CostEstimate(

time: 32.9 us -> 32 us (0.973)
  waiting for transfers between devices: 1.29 us -> 0.2 us
  starting transfers between devices: 18.2 us -> 18.8 us
    all_to_all x1, waiting for transfers between devices: 1.28 us -> 0.19 us  [on_device(): lax.all_to_all(send, 'ml', split_axis=0, concat_axis=0, tiled=True, axis_...]
    all_to_all x1, starting transfers between devices: 8.84 us -> 9.29 us  [on_device(): lax.all_to_all(send, 'ml', split_axis=0, concat_axis=0, tiled=True, axis_...]
where the time goes in v5:
time: 32 us; the launch traced here: 31.7 us
  starting transfers between devices  18.8 us (59%)
  Pallas kernels  11.4 us (36%)
  between operations  0.68 us (2%)
  local copies, waits for them, and re-layouts  0.62 us (2%)
    all_to_all x1, starting transfers between devices, on_device(): lax.all_to_all(send, 'ml', split_axis=0, concat_axis=0, tiled=True, axis_...  9.29 us
    all_to_all x1, starting transfers between devices, on_device(): lax.all_to_all(forces, 'ml', split_axis=0, concat_axis=0, tiled=True, axi...  6.39 us
    pallas_call x1, Pallas kernels, on_device(): pl.pallas_call(patch_kernel, out_shape=jax.ShapeDtypeStruct((own // share...  5.86 us
    pallas_call x1, Pallas kernels, on_device(): pl.pallas_call(pair_kernel, out_shape=jax.ShapeDtypeStruct((3, atom_count...  3.75 us
    ppermute x1, starting transfers between devices, on_device(): high = lax.ppermute(atoms, ('dom', 'ml'), backward)  3.1 us
    pallas_call x1, Pallas kernels, on_device(): pl.pallas_call(pack_kernel, out_shape=(jax.ShapeDtypeStruct((members, sha...  1.77 us
  transfers between devices with their start and end apart: 4, of which 1 were waited for; matrix products, arithmetic and copies ran while one was open for 0% of the time, Pallas kernels for 30%

profile of v5, /device:TPU:0, one launch (start us, length us, event | category | flops | bytes accessed | tf_op | source)
XLA Modules:
  0.0 31.7 jit_solution(2591316194760766676)
XLA Ops:
  0.6 1.8 %shard_map.113 = (bf16[16,48,128]{2,1,0:T(8,128)(2,1)}, f32[4,2048]{1,0:T(4,128)S(1)}, f32[2,8,128]{2,1,0:T(8,128)S(1)}) custom-call(bf16[8,32,128]{2,1,0:T(8,128)(2,1)} %feat_ref.1, f32[3,8,32]{2,1,0:T(8,128)} %bitcast.4, s32[8,32,32]{2,1,0:T(8,128)} %nb_ref.1, f32[3,2048]{1,0:T(4,128)} %mm_pos_ref.1, f32[1,2048]{1,0:T(1,128)} %bitcast.5, ...), custom_call_target="tpu_custom_call" | custom-call | flops 1000 | bytes 400000 | tf_op jit(solution)/shard_map/pallas_call | solution.py:344
  2.4 0.0 copy-start
  2.4 0.0 copy-start.1
  2.4 0.0 copy-start.2
  2.4 9.3 %all-to-all-start = ((bf16[16,48,128]{2,1,0:T(8,128)(2,1)}), bf16[16,48,128]{2,1,0:T(8,128)(2,1)S(1)}, u32[]{:S(2)}, u32[]{:S(2)}) async-start(bf16[16,48,128]{2,1,0:T(8,128)(2,1)} %get-tuple-element.6), calls=%async_computation | async-start | bytes 393216 | tf_op jit(solution)/shard_map/all_to_all | solution.py:363
  11.7 3.1 %collective-permute-start.1 = (f32[4,2048]{1,0:T(4,128)S(1)}, f32[4,2048]{1,0:T(4,128)S(1)}, u32[]{:S(2)}, u32[]{:S(2)}) collective-permute-start(f32[4,2048]{1,0:T(4,128)S(1)} %get-tuple-element.5.own_ref), channel_id=1, source_target_pairs={{1,0},{2,1},{3,2},{4,3},{5,4},{6,5},{7,6},{8,7},{9,8},{10,9},{11,1... | collective-permute-start | bytes 98312 | tf_op jit(solution)/shard_map/ppermute | solution.py:376
  14.8 0.0 collective-permute-start
  14.8 0.2 all-to-all-done.recv_ref
  15.0 0.0 copy-done
  15.0 0.0 copy-done.1
  15.0 0.0 copy-done.2
  15.0 5.9 %shard_map.115 = f32[8,8,128]{2,1,0:T(8,128)} custom-call(bf16[16,48,128]{2,1,0:T(8,128)(2,1)S(1)} %all-to-all-done.recv_ref, bf16[2,128,128]{2,1,0:T(8,128)(2,1)S(1)} %copy-done, f32[2,8,128]{2,1,0:T(8,128)S(1)} %get-tuple-element.7.radial_ref, bf16[2,128,128]{2,1,0:T(8,128)(2,1)S(1)} %copy-done.1, bf16[128,256]{1,0:T(8,128)(2,1)S(1)} %copy-done.2), custom_call_target="tpu_custom_call" | custom-call | flops 5000000000 | bytes 1000000 | tf_op jit(solution)/shard_map/pallas_call | solution.py:378
  20.9 0.0 copy-start.3
  20.9 6.4 %all-to-all-start.1 = ((f32[8,8,128]{2,1,0:T(8,128)}), f32[8,8,128]{2,1,0:T(8,128)S(1)}, u32[]{:S(2)}, u32[]{:S(2)}) async-start(f32[8,8,128]{2,1,0:T(8,128)} %shard_map.115), calls=%async_computation.1 | async-start | bytes 65536 | tf_op jit(solution)/shard_map/all_to_all | solution.py:404
  27.3 0.0 collective-permute-done.1.high_ref
  27.3 0.0 collective-permute-done.low_ref
  27.3 0.0 copy-done.3
  27.3 3.8 %shard_map.114 = f32[3,2048]{1,0:T(4,128)} custom-call(s32[8,16]{1,0:T(8,128)S(1)} %bitcast.3, f32[4,2048]{1,0:T(4,128)S(1)} %get-tuple-element.5.own_ref, f32[4,2048]{1,0:T(4,128)S(1)} %collective-permute-done.low_ref, f32[4,2048]{1,0:T(4,128)S(1)} %collective-permute-done.1.high_ref), custom_call_target="tpu_custom_call" | custom-call | flops 4000000000 | bytes 200000 | tf_op jit(solution)/shard_map/pallas_call | solution.py:409
  31.0 0.0 all-to-all-done.1
  31.1 0.6 %copy.12 = f32[8,3,32]{2,0,1:T(8,128)} copy(f32[8,3,32]{2,1,0:T(4,128)S(1)} %slice.4) | data formatting | bytes 6144
  (1 shorter events, 0.0 us)
Async XLA Ops:
  2.4 12.6 %copy-start = (bf16[2,128,128]{2,1,0:T(8,128)(2,1)S(1)}, bf16[2,128,128]{2,1,0:T(8,128)(2,1)}, u32[]{:S(2)}) copy-start(bf16[2,128,128]{2,1,0:T(8,128)(2,1)} %msg_ref.1) | copy-start | bytes 196612
  2.4 12.6 %copy-start.1 = (bf16[2,128,128]{2,1,0:T(8,128)(2,1)S(1)}, bf16[2,128,128]{2,1,0:T(8,128)(2,1)}, u32[]{:S(2)}) copy-start(bf16[2,128,128]{2,1,0:T(8,128)(2,1)} %out_w_ref.1) | copy-start | bytes 196612
  2.4 12.6 %copy-start.2 = (bf16[128,256]{1,0:T(8,128)(2,1)S(1)}, bf16[128,256]{1,0:T(8,128)(2,1)}, u32[]{:S(2)}) copy-start(bf16[128,256]{1,0:T(8,128)(2,1)} %read_ref.1) | copy-start | bytes 196612
  2.4 12.6 %all-to-all-start = ((bf16[16,48,128]{2,1,0:T(8,128)(2,1)}), bf16[16,48,128]{2,1,0:T(8,128)(2,1)S(1)}, u32[]{:S(2)}, u32[]{:S(2)}) async-start(bf16[16,48,128]{2,1,0:T(8,128)(2,1)} %get-tuple-element.6), calls=%async_computation | async-start | bytes 393216 | tf_op jit(solution)/shard_map/all_to_all | solution.py:363
  11.7 15.6 %collective-permute-start.1 = (f32[4,2048]{1,0:T(4,128)S(1)}, f32[4,2048]{1,0:T(4,128)S(1)}, u32[]{:S(2)}, u32[]{:S(2)}) collective-permute-start(f32[4,2048]{1,0:T(4,128)S(1)} %get-tuple-element.5.own_ref), channel_id=1, source_target_pairs={{1,0},{2,1},{3,2},{4,3},{5,4},{6,5},{7,6},{8,7},{9,8},{10,9},{11,1... | collective-permute-start | bytes 98312 | tf_op jit(solution)/shard_map/ppermute | solution.py:376
  14.8 12.5 %collective-permute-start = (f32[4,2048]{1,0:T(4,128)S(1)}, f32[4,2048]{1,0:T(4,128)S(1)}, u32[]{:S(2)}, u32[]{:S(2)}) collective-permute-start(f32[4,2048]{1,0:T(4,128)S(1)} %get-tuple-element.5.own_ref), channel_id=1, source_target_pairs={{0,1},{1,2},{2,3},{3,4},{4,5},{5,6},{6,7},{7,8},{8,9},{9,10},{10,1... | collective-permute-start | bytes 98312 | tf_op jit(solution)/shard_map/ppermute | solution.py:375
  20.9 6.4 %copy-start.3 = (s32[16,8]{0,1:T(8,128)S(1)}, s32[16,8]{0,1:T(8,128)}, u32[]{:S(2)}) copy-start(s32[16,8]{0,1:T(8,128)} %param.12) | copy-start | bytes 1540
  20.9 10.2 %all-to-all-start.1 = ((f32[8,8,128]{2,1,0:T(8,128)}), f32[8,8,128]{2,1,0:T(8,128)S(1)}, u32[]{:S(2)}, u32[]{:S(2)}) async-start(f32[8,8,128]{2,1,0:T(8,128)} %shard_map.115), calls=%async_computation.1 | async-start | bytes 65536 | tf_op jit(solution)/shard_map/all_to_all | solution.py:404

commit v6 on v5

--- a/solution.py
+++ b/solution.py
@@ -12,6 +12,8 @@
 SOFTEN = 1.0
 COULOMB = 0.5
 HALVES = 2
+FIELDS = 5
+BITS = 6
 
 
 FIRST = {16: 10, 8: 2}
@@ -167,13 +169,17 @@
     square_ref[...] = jnp.dot(mine_ref[...], near_ref[...], preferred_element_type=F32)
 
     index = low_ref[...]
-    low_ref[...] = index & 127
-    unit_ref[...] = jnp.int32(1) << ((index >> 7) << 3)
-    rows = lax.broadcasted_iota(jnp.int32, (128, 128), 0)
+    depth = count_ref.shape[0]
+    field = jnp.zeros_like(index)
+    for f in range(1, FIELDS):
+        field += (index >= depth * f).astype(jnp.int32)
+    low_ref[...] = index - field * depth
+    unit_ref[...] = jnp.int32(1) << (field * BITS)
+    rows = lax.broadcasted_iota(jnp.int32, (depth, 128), 0)
 
     def count(b):
         lanes = slice(128 * b, 128 * (b + 1))
-        total = jnp.zeros((128, 128), jnp.int32)
+        total = jnp.zeros((depth, 128), jnp.int32)
         for k in range(neighbours):
             total += jnp.where(rows == low_ref[k : k + 1, lanes], unit_ref[k : k + 1, lanes], 0)
         count_ref[:, lanes] = total
@@ -186,8 +192,12 @@
     def pairs(lanes):
         for s in range(size // step):
             here = slice(step * s, step * (s + 1))
-            f, first = divmod(step * s, 128)
-            times = ((count_ref[first : first + step, lanes] >> (8 * f)) & 255).astype(F32)
+            found = []
+            for group in range(0, step, 8):
+                f, first = divmod(step * s + group, depth)
+                packed = count_ref[first : first + 8, lanes]
+                found.append((packed >> (BITS * f)) & ((1 << BITS) - 1))
+            times = jnp.concatenate(found, axis=0).astype(F32)
             near = jnp.minimum(square_ref[here, lanes], limit)
             root = series[-1]
             for value in series[-2::-1]:
@@ -390,7 +400,7 @@
             pltpu.VMEM((16, size), BF16),
             pltpu.VMEM((neighbours, size), jnp.int32),
             pltpu.VMEM((neighbours, size), jnp.int32),
-            pltpu.VMEM((128, size), jnp.int32),
+            pltpu.VMEM((-(-size // (8 * FIELDS)) * 8, size), jnp.int32),
             pltpu.VMEM((size, size), F32),
             pltpu.VMEM((basis_count, size, size), BF16),
             pltpu.VMEM((size, size), F32),

time: 32 us -> 31.8 us (level)
  no operation moved by 1% of the time
where the time goes in v6:
time: 31.8 us; the launch traced here: 31.5 us
  starting transfers between devices  18.8 us (59%)
  Pallas kernels  11.2 us (35%)
  between operations  0.68 us (2%)
  local copies, waits for them, and re-layouts  0.62 us (2%)
    all_to_all x1, starting transfers between devices, on_device(): lax.all_to_all(send, 'ml', split_axis=0, concat_axis=0, tiled=True, axis_...  9.29 us
    all_to_all x1, starting transfers between devices, on_device(): lax.all_to_all(forces, 'ml', split_axis=0, concat_axis=0, tiled=True, axi...  6.4 us
    pallas_call x1, Pallas kernels, on_device(): pl.pallas_call(patch_kernel, out_shape=jax.ShapeDtypeStruct((own // share...  5.65 us
    pallas_call x1, Pallas kernels, on_device(): pl.pallas_call(pair_kernel, out_shape=jax.ShapeDtypeStruct((3, atom_count...  3.75 us
    ppermute x1, starting transfers between devices, on_device(): high = lax.ppermute(atoms, ('dom', 'ml'), backward)  3.1 us
    pallas_call x1, Pallas kernels, on_device(): pl.pallas_call(pack_kernel, out_shape=(jax.ShapeDtypeStruct((members, sha...  1.77 us
  transfers between devices with their start and end apart: 4, of which 1 were waited for; matrix products, arithmetic and copies ran while one was open for 0% of the time, Pallas kernels for 30%

profile of v6, /device:TPU:0, one launch (start us, length us, event | category | flops | bytes accessed | tf_op | source)
XLA Modules:
  0.0 31.5 jit_solution(16918373115120204622)
XLA Ops:
  0.6 1.8 %shard_map.113 = (bf16[16,48,128]{2,1,0:T(8,128)(2,1)}, f32[4,2048]{1,0:T(4,128)S(1)}, f32[2,8,128]{2,1,0:T(8,128)S(1)}) custom-call(bf16[8,32,128]{2,1,0:T(8,128)(2,1)} %feat_ref.1, f32[3,8,32]{2,1,0:T(8,128)} %bitcast.4, s32[8,32,32]{2,1,0:T(8,128)} %nb_ref.1, f32[3,2048]{1,0:T(4,128)} %mm_pos_ref.1, f32[1,2048]{1,0:T(1,128)} %bitcast.5, ...), custom_call_target="tpu_custom_call" | custom-call | flops 1000 | bytes 400000 | tf_op jit(solution)/shard_map/pallas_call | solution.py:354
  2.4 0.0 copy-start
  2.4 0.0 copy-start.1
  2.4 0.0 copy-start.2
  2.4 9.3 %all-to-all-start = ((bf16[16,48,128]{2,1,0:T(8,128)(2,1)}), bf16[16,48,128]{2,1,0:T(8,128)(2,1)S(1)}, u32[]{:S(2)}, u32[]{:S(2)}) async-start(bf16[16,48,128]{2,1,0:T(8,128)(2,1)} %get-tuple-element.6), calls=%async_computation | async-start | bytes 393216 | tf_op jit(solution)/shard_map/all_to_all | solution.py:373
  11.7 3.1 %collective-permute-start.1 = (f32[4,2048]{1,0:T(4,128)S(1)}, f32[4,2048]{1,0:T(4,128)S(1)}, u32[]{:S(2)}, u32[]{:S(2)}) collective-permute-start(f32[4,2048]{1,0:T(4,128)S(1)} %get-tuple-element.5.own_ref), channel_id=1, source_target_pairs={{1,0},{2,1},{3,2},{4,3},{5,4},{6,5},{7,6},{8,7},{9,8},{10,9},{11,1... | collective-permute-start | bytes 98312 | tf_op jit(solution)/shard_map/ppermute | solution.py:386
  14.8 0.0 collective-permute-start
  14.8 0.2 all-to-all-done.recv_ref
  15.0 0.0 copy-done
  15.0 0.0 copy-done.1
  15.0 0.0 copy-done.2
  15.0 5.7 %shard_map.115 = f32[8,8,128]{2,1,0:T(8,128)} custom-call(bf16[16,48,128]{2,1,0:T(8,128)(2,1)S(1)} %all-to-all-done.recv_ref, bf16[2,128,128]{2,1,0:T(8,128)(2,1)S(1)} %copy-done, f32[2,8,128]{2,1,0:T(8,128)S(1)} %get-tuple-element.7.radial_ref, bf16[2,128,128]{2,1,0:T(8,128)(2,1)S(1)} %copy-done.1, bf16[128,256]{1,0:T(8,128)(2,1)S(1)} %copy-done.2), custom_call_target="tpu_custom_call" | custom-call | flops 5000000000 | bytes 1000000 | tf_op jit(solution)/shard_map/pallas_call | solution.py:388
  20.7 0.0 copy-start.3
  20.7 6.4 %all-to-all-start.1 = ((f32[8,8,128]{2,1,0:T(8,128)}), f32[8,8,128]{2,1,0:T(8,128)S(1)}, u32[]{:S(2)}, u32[]{:S(2)}) async-start(f32[8,8,128]{2,1,0:T(8,128)} %shard_map.115), calls=%async_computation.1 | async-start | bytes 65536 | tf_op jit(solution)/shard_map/all_to_all | solution.py:414
  27.1 0.0 collective-permute-done.1.high_ref
  27.1 0.0 collective-permute-done.low_ref
  27.1 0.0 copy-done.3
  27.1 3.8 %shard_map.114 = f32[3,2048]{1,0:T(4,128)} custom-call(s32[8,16]{1,0:T(8,128)S(1)} %bitcast.3, f32[4,2048]{1,0:T(4,128)S(1)} %get-tuple-element.5.own_ref, f32[4,2048]{1,0:T(4,128)S(1)} %collective-permute-done.low_ref, f32[4,2048]{1,0:T(4,128)S(1)} %collective-permute-done.1.high_ref), custom_call_target="tpu_custom_call" | custom-call | flops 4000000000 | bytes 200000 | tf_op jit(solution)/shard_map/pallas_call | solution.py:419
  30.8 0.0 all-to-all-done.1
  30.9 0.6 %copy.12 = f32[8,3,32]{2,0,1:T(8,128)} copy(f32[8,3,32]{2,1,0:T(4,128)S(1)} %slice.4) | data formatting | bytes 6144
  (1 shorter events, 0.0 us)
Async XLA Ops:
  2.4 12.6 %copy-start = (bf16[2,128,128]{2,1,0:T(8,128)(2,1)S(1)}, bf16[2,128,128]{2,1,0:T(8,128)(2,1)}, u32[]{:S(2)}) copy-start(bf16[2,128,128]{2,1,0:T(8,128)(2,1)} %msg_ref.1) | copy-start | bytes 196612
  2.4 12.6 %copy-start.1 = (bf16[2,128,128]{2,1,0:T(8,128)(2,1)S(1)}, bf16[2,128,128]{2,1,0:T(8,128)(2,1)}, u32[]{:S(2)}) copy-start(bf16[2,128,128]{2,1,0:T(8,128)(2,1)} %out_w_ref.1) | copy-start | bytes 196612
  2.4 12.6 %copy-start.2 = (bf16[128,256]{1,0:T(8,128)(2,1)S(1)}, bf16[128,256]{1,0:T(8,128)(2,1)}, u32[]{:S(2)}) copy-start(bf16[128,256]{1,0:T(8,128)(2,1)} %read_ref.1) | copy-start | bytes 196612
  2.4 12.6 %all-to-all-start = ((bf16[16,48,128]{2,1,0:T(8,128)(2,1)}), bf16[16,48,128]{2,1,0:T(8,128)(2,1)S(1)}, u32[]{:S(2)}, u32[]{:S(2)}) async-start(bf16[16,48,128]{2,1,0:T(8,128)(2,1)} %get-tuple-element.6), calls=%async_computation | async-start | bytes 393216 | tf_op jit(solution)/shard_map/all_to_all | solution.py:373
  11.7 15.4 %collective-permute-start.1 = (f32[4,2048]{1,0:T(4,128)S(1)}, f32[4,2048]{1,0:T(4,128)S(1)}, u32[]{:S(2)}, u32[]{:S(2)}) collective-permute-start(f32[4,2048]{1,0:T(4,128)S(1)} %get-tuple-element.5.own_ref), channel_id=1, source_target_pairs={{1,0},{2,1},{3,2},{4,3},{5,4},{6,5},{7,6},{8,7},{9,8},{10,9},{11,1... | collective-permute-start | bytes 98312 | tf_op jit(solution)/shard_map/ppermute | solution.py:386
  14.8 12.3 %collective-permute-start = (f32[4,2048]{1,0:T(4,128)S(1)}, f32[4,2048]{1,0:T(4,128)S(1)}, u32[]{:S(2)}, u32[]{:S(2)}) collective-permute-start(f32[4,2048]{1,0:T(4,128)S(1)} %get-tuple-element.5.own_ref), channel_id=1, source_target_pairs={{0,1},{1,2},{2,3},{3,4},{4,5},{5,6},{6,7},{7,8},{8,9},{9,10},{10,1... | collective-permute-start | bytes 98312 | tf_op jit(solution)/shard_map/ppermute | solution.py:385
  20.7 6.4 %copy-start.3 = (s32[16,8]{0,1:T(8,128)S(1)}, s32[16,8]{0,1:T(8,128)}, u32[]{:S(2)}) copy-start(s32[16,8]{0,1:T(8,128)} %param.12) | copy-start | bytes 1540
  20.7 10.2 %all-to-all-start.1 = ((f32[8,8,128]{2,1,0:T(8,128)}), f32[8,8,128]{2,1,0:T(8,128)S(1)}, u32[]{:S(2)}, u32[]{:S(2)}) async-start(f32[8,8,128]{2,1,0:T(8,128)} %shard_map.115), calls=%async_computation.1 | async-start | bytes 65536 | tf_op jit(solution)/shard_map/all_to_all | solution.py:414

commit v7 on v6

--- a/solution.py
+++ b/solution.py
@@ -16,7 +16,7 @@
 BITS = 6
 
 
-FIRST = {16: 10, 8: 2}
+FIRST = {16: 11, 8: 2}
 
 
 def exchange_order(count):

time: 31.8 us -> 31.7 us (level)
  starting transfers between devices: 18.8 us -> 17.6 us
  waiting for transfers between devices: 0.2 us -> 1.14 us
    all_to_all x1, starting transfers between devices: 6.4 us -> 5.43 us  [on_device(): lax.all_to_all(forces, 'ml', split_axis=0, concat_axis=0, tiled=True, axi...]
    all_to_all x1, waiting for transfers between devices: 0.19 us -> 1.13 us  [on_device(): lax.all_to_all(send, 'ml', split_axis=0, concat_axis=0, tiled=True, axis_...]
where the time goes in v7:
time: 31.7 us; the launch traced here: 31.3 us
  starting transfers between devices  17.6 us (56%)
  Pallas kernels  11.2 us (35%)
  waiting for transfers between devices  1.14 us (4%)
  between operations  0.68 us (2%)
  local copies, waits for them, and re-layouts  0.62 us (2%)
    all_to_all x1, starting transfers between devices, on_device(): lax.all_to_all(send, 'ml', split_axis=0, concat_axis=0, tiled=True, axis_...  9.11 us
    pallas_call x1, Pallas kernels, on_device(): pl.pallas_call(patch_kernel, out_shape=jax.ShapeDtypeStruct((own // share...  5.65 us
    all_to_all x1, starting transfers between devices, on_device(): lax.all_to_all(forces, 'ml', split_axis=0, concat_axis=0, tiled=True, axi...  5.43 us
    pallas_call x1, Pallas kernels, on_device(): pl.pallas_call(pair_kernel, out_shape=jax.ShapeDtypeStruct((3, atom_count...  3.75 us
    ppermute x1, starting transfers between devices, on_device(): high = lax.ppermute(atoms, ('dom', 'ml'), backward)  3.1 us
    pallas_call x1, Pallas kernels, on_device(): pl.pallas_call(pack_kernel, out_shape=(jax.ShapeDtypeStruct((members, sha...  1.77 us
    all_to_all x1, waiting for transfers between devices, on_device(): lax.all_to_all(send, 'ml', split_axis=0, concat_axis=0, tiled=True, axis_...  1.13 us
  transfers between devices with their start and end apart: 4, of which 1 were waited for; matrix products, arithmetic and copies ran while one was open for 0% of the time, Pallas kernels for 30%

profile of v7, /device:TPU:0, one launch (start us, length us, event | category | flops | bytes accessed | tf_op | source)
XLA Modules:
  0.0 31.3 jit_solution(4328485236613809411)
XLA Ops:
  0.6 1.8 %shard_map.113 = (bf16[16,48,128]{2,1,0:T(8,128)(2,1)}, f32[4,2048]{1,0:T(4,128)S(1)}, f32[2,8,128]{2,1,0:T(8,128)S(1)}) custom-call(bf16[8,32,128]{2,1,0:T(8,128)(2,1)} %feat_ref.1, f32[3,8,32]{2,1,0:T(8,128)} %bitcast.4, s32[8,32,32]{2,1,0:T(8,128)} %nb_ref.1, f32[3,2048]{1,0:T(4,128)} %mm_pos_ref.1, f32[1,2048]{1,0:T(1,128)} %bitcast.5, ...), custom_call_target="tpu_custom_call" | custom-call | flops 1000 | bytes 400000 | tf_op jit(solution)/shard_map/pallas_call | solution.py:354
  2.4 0.0 copy-start
  2.4 0.0 copy-start.1
  2.4 0.0 copy-start.2
  2.4 9.1 %all-to-all-start = ((bf16[16,48,128]{2,1,0:T(8,128)(2,1)}), bf16[16,48,128]{2,1,0:T(8,128)(2,1)S(1)}, u32[]{:S(2)}, u32[]{:S(2)}) async-start(bf16[16,48,128]{2,1,0:T(8,128)(2,1)} %get-tuple-element.6), calls=%async_computation | async-start | bytes 393216 | tf_op jit(solution)/shard_map/all_to_all | solution.py:373
  11.5 3.1 %collective-permute-start.1 = (f32[4,2048]{1,0:T(4,128)S(1)}, f32[4,2048]{1,0:T(4,128)S(1)}, u32[]{:S(2)}, u32[]{:S(2)}) collective-permute-start(f32[4,2048]{1,0:T(4,128)S(1)} %get-tuple-element.5.own_ref), channel_id=1, source_target_pairs={{1,0},{2,1},{3,2},{4,3},{5,4},{6,5},{7,6},{8,7},{9,8},{10,9},{11,1... | collective-permute-start | bytes 98312 | tf_op jit(solution)/shard_map/ppermute | solution.py:386
  14.6 0.0 collective-permute-start
  14.6 1.1 %all-to-all-done.recv_ref = bf16[16,48,128]{2,1,0:T(8,128)(2,1)S(1)} async-done(((bf16[16,48,128]{2,1,0:T(8,128)(2,1)}), bf16[16,48,128]{2,1,0:T(8,128)(2,1)S(1)}, u32[]{:S(2)}, u32[]{:S(2)}) %all-to-all-start) | async-done | bytes 196640 | tf_op jit(solution)/shard_map/all_to_all | solution.py:373
  15.8 0.0 copy-done
  15.8 0.0 copy-done.1
  15.8 0.0 copy-done.2
  15.8 5.7 %shard_map.115 = f32[8,8,128]{2,1,0:T(8,128)} custom-call(bf16[16,48,128]{2,1,0:T(8,128)(2,1)S(1)} %all-to-all-done.recv_ref, bf16[2,128,128]{2,1,0:T(8,128)(2,1)S(1)} %copy-done, f32[2,8,128]{2,1,0:T(8,128)S(1)} %get-tuple-element.7.radial_ref, bf16[2,128,128]{2,1,0:T(8,128)(2,1)S(1)} %copy-done.1, bf16[128,256]{1,0:T(8,128)(2,1)S(1)} %copy-done.2), custom_call_target="tpu_custom_call" | custom-call | flops 5000000000 | bytes 1000000 | tf_op jit(solution)/shard_map/pallas_call | solution.py:388
  21.4 0.0 copy-start.3
  21.4 5.4 %all-to-all-start.1 = ((f32[8,8,128]{2,1,0:T(8,128)}), f32[8,8,128]{2,1,0:T(8,128)S(1)}, u32[]{:S(2)}, u32[]{:S(2)}) async-start(f32[8,8,128]{2,1,0:T(8,128)} %shard_map.115), calls=%async_computation.1 | async-start | bytes 65536 | tf_op jit(solution)/shard_map/all_to_all | solution.py:414
  26.9 0.0 collective-permute-done.1.high_ref
  26.9 0.0 collective-permute-done.low_ref
  26.9 0.0 copy-done.3
  26.9 3.8 %shard_map.114 = f32[3,2048]{1,0:T(4,128)} custom-call(s32[8,16]{1,0:T(8,128)S(1)} %bitcast.3, f32[4,2048]{1,0:T(4,128)S(1)} %get-tuple-element.5.own_ref, f32[4,2048]{1,0:T(4,128)S(1)} %collective-permute-done.low_ref, f32[4,2048]{1,0:T(4,128)S(1)} %collective-permute-done.1.high_ref), custom_call_target="tpu_custom_call" | custom-call | flops 4000000000 | bytes 200000 | tf_op jit(solution)/shard_map/pallas_call | solution.py:419
  30.6 0.0 all-to-all-done.1
  30.7 0.6 %copy.12 = f32[8,3,32]{2,0,1:T(8,128)} copy(f32[8,3,32]{2,1,0:T(4,128)S(1)} %slice.4) | data formatting | bytes 6144
  (1 shorter events, 0.0 us)
Async XLA Ops:
  2.4 13.4 %copy-start = (bf16[2,128,128]{2,1,0:T(8,128)(2,1)S(1)}, bf16[2,128,128]{2,1,0:T(8,128)(2,1)}, u32[]{:S(2)}) copy-start(bf16[2,128,128]{2,1,0:T(8,128)(2,1)} %msg_ref.1) | copy-start | bytes 196612
  2.4 13.4 %copy-start.1 = (bf16[2,128,128]{2,1,0:T(8,128)(2,1)S(1)}, bf16[2,128,128]{2,1,0:T(8,128)(2,1)}, u32[]{:S(2)}) copy-start(bf16[2,128,128]{2,1,0:T(8,128)(2,1)} %out_w_ref.1) | copy-start | bytes 196612
  2.4 13.4 %copy-start.2 = (bf16[128,256]{1,0:T(8,128)(2,1)S(1)}, bf16[128,256]{1,0:T(8,128)(2,1)}, u32[]{:S(2)}) copy-start(bf16[128,256]{1,0:T(8,128)(2,1)} %read_ref.1) | copy-start | bytes 196612
  2.4 13.3 %all-to-all-start = ((bf16[16,48,128]{2,1,0:T(8,128)(2,1)}), bf16[16,48,128]{2,1,0:T(8,128)(2,1)S(1)}, u32[]{:S(2)}, u32[]{:S(2)}) async-start(bf16[16,48,128]{2,1,0:T(8,128)(2,1)} %get-tuple-element.6), calls=%async_computation | async-start | bytes 393216 | tf_op jit(solution)/shard_map/all_to_all | solution.py:373
  11.5 15.3 %collective-permute-start.1 = (f32[4,2048]{1,0:T(4,128)S(1)}, f32[4,2048]{1,0:T(4,128)S(1)}, u32[]{:S(2)}, u32[]{:S(2)}) collective-permute-start(f32[4,2048]{1,0:T(4,128)S(1)} %get-tuple-element.5.own_ref), channel_id=1, source_target_pairs={{1,0},{2,1},{3,2},{4,3},{5,4},{6,5},{7,6},{8,7},{9,8},{10,9},{11,1... | collective-permute-start | bytes 98312 | tf_op jit(solution)/shard_map/ppermute | solution.py:386
  14.6 12.2 %collective-permute-start = (f32[4,2048]{1,0:T(4,128)S(1)}, f32[4,2048]{1,0:T(4,128)S(1)}, u32[]{:S(2)}, u32[]{:S(2)}) collective-permute-start(f32[4,2048]{1,0:T(4,128)S(1)} %get-tuple-element.5.own_ref), channel_id=1, source_target_pairs={{0,1},{1,2},{2,3},{3,4},{4,5},{5,6},{6,7},{7,8},{8,9},{9,10},{10,1... | collective-permute-start | bytes 98312 | tf_op jit(solution)/shard_map/ppermute | solution.py:385
  21.4 5.4 %copy-start.3 = (s32[16,8]{0,1:T(8,128)S(1)}, s32[16,8]{0,1:T(8,128)}, u32[]{:S(2)}) copy-start(s32[16,8]{0,1:T(8,128)} %param.12) | copy-start | bytes 1540
  21.4 9.2 %all-to-all-start.1 = ((f32[8,8,128]{2,1,0:T(8,128)}), f32[8,8,128]{2,1,0:T(8,128)S(1)}, u32[]{:S(2)}, u32[]{:S(2)}) async-start(f32[8,8,128]{2,1,0:T(8,128)} %shard_map.115), calls=%async_computation.1 | async-start | bytes 65536 | tf_op jit(solution)/shard_map/all_to_all | solution.py:414

commit v8 on v7

--- a/solution.py
+++ b/solution.py
@@ -17,9 +17,12 @@
 
 
 FIRST = {16: 11, 8: 2}
+EIGHT = (2, 3, 6, 0, 7, 4, 5, 1)
 
 
 def exchange_order(count):
+    if count == len(EIGHT):
+        return list(EIGHT)
     first = FIRST.get(count, count - 1)
     return [first] + [member for member in range(count)[::-1] if member != first]
 

time: 31.7 us -> 31.7 us (level)
  no operation moved by 1% of the time
where the time goes in v8:
time: 31.7 us; the launch traced here: 31.3 us
  starting transfers between devices  17.6 us (56%)
  Pallas kernels  11.2 us (35%)
  waiting for transfers between devices  1.14 us (4%)
  between operations  0.68 us (2%)
  local copies, waits for them, and re-layouts  0.62 us (2%)
    all_to_all x1, starting transfers between devices, on_device(): lax.all_to_all(send, 'ml', split_axis=0, concat_axis=0, tiled=True, axis_...  9.11 us
    pallas_call x1, Pallas kernels, on_device(): pl.pallas_call(patch_kernel, out_shape=jax.ShapeDtypeStruct((own // share...  5.65 us
    all_to_all x1, starting transfers between devices, on_device(): lax.all_to_all(forces, 'ml', split_axis=0, concat_axis=0, tiled=True, axi...  5.43 us
    pallas_call x1, Pallas kernels, on_device(): pl.pallas_call(pair_kernel, out_shape=jax.ShapeDtypeStruct((3, atom_count...  3.75 us
    ppermute x1, starting transfers between devices, on_device(): high = lax.ppermute(atoms, ('dom', 'ml'), backward)  3.1 us
    pallas_call x1, Pallas kernels, on_device(): pl.pallas_call(pack_kernel, out_shape=(jax.ShapeDtypeStruct((members, sha...  1.77 us
    all_to_all x1, waiting for transfers between devices, on_device(): lax.all_to_all(send, 'ml', split_axis=0, concat_axis=0, tiled=True, axis_...  1.13 us
  transfers between devices with their start and end apart: 4, of which 1 were waited for; matrix products, arithmetic and copies ran while one was open for 0% of the time, Pallas kernels for 30%

profile of v8, /device:TPU:0, one launch (start us, length us, event | category | flops | bytes accessed | tf_op | source)
XLA Modules:
  0.0 31.3 jit_solution(17966192337531427258)
XLA Ops:
  0.6 1.8 %shard_map.113 = (bf16[16,48,128]{2,1,0:T(8,128)(2,1)}, f32[4,2048]{1,0:T(4,128)S(1)}, f32[2,8,128]{2,1,0:T(8,128)S(1)}) custom-call(bf16[8,32,128]{2,1,0:T(8,128)(2,1)} %feat_ref.1, f32[3,8,32]{2,1,0:T(8,128)} %bitcast.4, s32[8,32,32]{2,1,0:T(8,128)} %nb_ref.1, f32[3,2048]{1,0:T(4,128)} %mm_pos_ref.1, f32[1,2048]{1,0:T(1,128)} %bitcast.5, ...), custom_call_target="tpu_custom_call" | custom-call | flops 1000 | bytes 400000 | tf_op jit(solution)/shard_map/pallas_call | solution.py:357
  2.4 0.0 copy-start
  2.4 0.0 copy-start.1
  2.4 0.0 copy-start.2
  2.4 9.1 %all-to-all-start = ((bf16[16,48,128]{2,1,0:T(8,128)(2,1)}), bf16[16,48,128]{2,1,0:T(8,128)(2,1)S(1)}, u32[]{:S(2)}, u32[]{:S(2)}) async-start(bf16[16,48,128]{2,1,0:T(8,128)(2,1)} %get-tuple-element.6), calls=%async_computation | async-start | bytes 393216 | tf_op jit(solution)/shard_map/all_to_all | solution.py:376
  11.5 3.1 %collective-permute-start.1 = (f32[4,2048]{1,0:T(4,128)S(1)}, f32[4,2048]{1,0:T(4,128)S(1)}, u32[]{:S(2)}, u32[]{:S(2)}) collective-permute-start(f32[4,2048]{1,0:T(4,128)S(1)} %get-tuple-element.5.own_ref), channel_id=1, source_target_pairs={{1,0},{2,1},{3,2},{4,3},{5,4},{6,5},{7,6},{8,7},{9,8},{10,9},{11,1... | collective-permute-start | bytes 98312 | tf_op jit(solution)/shard_map/ppermute | solution.py:389
  14.6 0.0 collective-permute-start
  14.6 1.1 %all-to-all-done.recv_ref = bf16[16,48,128]{2,1,0:T(8,128)(2,1)S(1)} async-done(((bf16[16,48,128]{2,1,0:T(8,128)(2,1)}), bf16[16,48,128]{2,1,0:T(8,128)(2,1)S(1)}, u32[]{:S(2)}, u32[]{:S(2)}) %all-to-all-start) | async-done | bytes 196640 | tf_op jit(solution)/shard_map/all_to_all | solution.py:376
  15.8 0.0 copy-done
  15.8 0.0 copy-done.1
  15.8 0.0 copy-done.2
  15.8 5.7 %shard_map.115 = f32[8,8,128]{2,1,0:T(8,128)} custom-call(bf16[16,48,128]{2,1,0:T(8,128)(2,1)S(1)} %all-to-all-done.recv_ref, bf16[2,128,128]{2,1,0:T(8,128)(2,1)S(1)} %copy-done, f32[2,8,128]{2,1,0:T(8,128)S(1)} %get-tuple-element.7.radial_ref, bf16[2,128,128]{2,1,0:T(8,128)(2,1)S(1)} %copy-done.1, bf16[128,256]{1,0:T(8,128)(2,1)S(1)} %copy-done.2), custom_call_target="tpu_custom_call" | custom-call | flops 5000000000 | bytes 1000000 | tf_op jit(solution)/shard_map/pallas_call | solution.py:391
  21.4 0.0 copy-start.3
  21.4 5.4 %all-to-all-start.1 = ((f32[8,8,128]{2,1,0:T(8,128)}), f32[8,8,128]{2,1,0:T(8,128)S(1)}, u32[]{:S(2)}, u32[]{:S(2)}) async-start(f32[8,8,128]{2,1,0:T(8,128)} %shard_map.115), calls=%async_computation.1 | async-start | bytes 65536 | tf_op jit(solution)/shard_map/all_to_all | solution.py:417
  26.9 0.0 collective-permute-done.1.high_ref
  26.9 0.0 collective-permute-done.low_ref
  26.9 0.0 copy-done.3
  26.9 3.8 %shard_map.114 = f32[3,2048]{1,0:T(4,128)} custom-call(s32[8,16]{1,0:T(8,128)S(1)} %bitcast.3, f32[4,2048]{1,0:T(4,128)S(1)} %get-tuple-element.5.own_ref, f32[4,2048]{1,0:T(4,128)S(1)} %collective-permute-done.low_ref, f32[4,2048]{1,0:T(4,128)S(1)} %collective-permute-done.1.high_ref), custom_call_target="tpu_custom_call" | custom-call | flops 4000000000 | bytes 200000 | tf_op jit(solution)/shard_map/pallas_call | solution.py:422
  30.6 0.0 all-to-all-done.1
  30.7 0.6 %copy.12 = f32[8,3,32]{2,0,1:T(8,128)} copy(f32[8,3,32]{2,1,0:T(4,128)S(1)} %slice.4) | data formatting | bytes 6144
  (1 shorter events, 0.0 us)
Async XLA Ops:
  2.4 13.4 %copy-start = (bf16[2,128,128]{2,1,0:T(8,128)(2,1)S(1)}, bf16[2,128,128]{2,1,0:T(8,128)(2,1)}, u32[]{:S(2)}) copy-start(bf16[2,128,128]{2,1,0:T(8,128)(2,1)} %msg_ref.1) | copy-start | bytes 196612
  2.4 13.4 %copy-start.1 = (bf16[2,128,128]{2,1,0:T(8,128)(2,1)S(1)}, bf16[2,128,128]{2,1,0:T(8,128)(2,1)}, u32[]{:S(2)}) copy-start(bf16[2,128,128]{2,1,0:T(8,128)(2,1)} %out_w_ref.1) | copy-start | bytes 196612
  2.4 13.4 %copy-start.2 = (bf16[128,256]{1,0:T(8,128)(2,1)S(1)}, bf16[128,256]{1,0:T(8,128)(2,1)}, u32[]{:S(2)}) copy-start(bf16[128,256]{1,0:T(8,128)(2,1)} %read_ref.1) | copy-start | bytes 196612
  2.4 13.3 %all-to-all-start = ((bf16[16,48,128]{2,1,0:T(8,128)(2,1)}), bf16[16,48,128]{2,1,0:T(8,128)(2,1)S(1)}, u32[]{:S(2)}, u32[]{:S(2)}) async-start(bf16[16,48,128]{2,1,0:T(8,128)(2,1)} %get-tuple-element.6), calls=%async_computation | async-start | bytes 393216 | tf_op jit(solution)/shard_map/all_to_all | solution.py:376
  11.5 15.3 %collective-permute-start.1 = (f32[4,2048]{1,0:T(4,128)S(1)}, f32[4,2048]{1,0:T(4,128)S(1)}, u32[]{:S(2)}, u32[]{:S(2)}) collective-permute-start(f32[4,2048]{1,0:T(4,128)S(1)} %get-tuple-element.5.own_ref), channel_id=1, source_target_pairs={{1,0},{2,1},{3,2},{4,3},{5,4},{6,5},{7,6},{8,7},{9,8},{10,9},{11,1... | collective-permute-start | bytes 98312 | tf_op jit(solution)/shard_map/ppermute | solution.py:389
  14.6 12.2 %collective-permute-start = (f32[4,2048]{1,0:T(4,128)S(1)}, f32[4,2048]{1,0:T(4,128)S(1)}, u32[]{:S(2)}, u32[]{:S(2)}) collective-permute-start(f32[4,2048]{1,0:T(4,128)S(1)} %get-tuple-element.5.own_ref), channel_id=1, source_target_pairs={{0,1},{1,2},{2,3},{3,4},{4,5},{5,6},{6,7},{7,8},{8,9},{9,10},{10,1... | collective-permute-start | bytes 98312 | tf_op jit(solution)/shard_map/ppermute | solution.py:388
  21.4 5.4 %copy-start.3 = (s32[16,8]{0,1:T(8,128)S(1)}, s32[16,8]{0,1:T(8,128)}, u32[]{:S(2)}) copy-start(s32[16,8]{0,1:T(8,128)} %param.12) | copy-start | bytes 1540
  21.4 9.2 %all-to-all-start.1 = ((f32[8,8,128]{2,1,0:T(8,128)}), f32[8,8,128]{2,1,0:T(8,128)S(1)}, u32[]{:S(2)}, u32[]{:S(2)}) async-start(f32[8,8,128]{2,1,0:T(8,128)} %shard_map.115), calls=%async_computation.1 | async-start | bytes 65536 | tf_op jit(solution)/shard_map/all_to_all | solution.py:417
